TPU v7x, 32 devices: a whole 2x2x4 slice. The times are simulated.
32 devices in a mesh: depth: 4 (over z), tile: 8 (over y, x, core).
Axes of the slice: x: 2, y: 2, z: 4, core: 2. Of those that a mesh axis runs over, the one named last changes fastest.
Arguments:
- transmission: float32 [2, 8, 2048, 512], P(None, 'depth', 'tile'), may hold values from -0.6 to 1.25, as said below
- probe: float32 [2, 256, 256], replicated, may hold values from -4.2 to 4.2
- intensity: float32 [16, 256, 256], P('tile'), may hold values from 0.25 to 4
- positions: int32 [16, 2], P('tile'), may hold values from 0 to 1792, as said below
- batch: int32 [16], P('tile'), may hold values from 0 to 1
Outputs:
- updated: float32 [2, 8, 2048, 512], P(None, 'depth', 'tile')
Inputs may be any that keep to these rules, and one draw needn't show every extreme that they name: `positions`: probe j is held by tile device j // 2; its top row minus 256 times that device's index, plus half of 256, lies between 0 and 255; its left column is at most 256. On every tile device the window of its first probe starts at least 64 rows above the device's rows (unless clipped at the object's top) and the window of its second probe ends at least 64 rows below them (unless clipped at the object's bottom). `transmission`: the first component lies between 0.5 and 1.25, the second between -0.6 and 0.6.
All inputs are finite; a program needn't handle non-finite values.
Results may differ from a plain program's by a relative error of at most 0.0003.
Values sent between devices are 32-bit elements; how exact they have to be, the bound alone decides.
A program may use at most 192 MiB of HBM per device.

v0:
```python
import math

import jax
import jax.numpy as jnp
from jax import lax
from jax.sharding import PartitionSpec as P

prop_strength = 24.0
step_rate = 0.08


def from_behind(value, axis, steps):
    count = lax.axis_size(axis)
    first, last = (max(0, -steps), min(count, count - steps))
    return lax.ppermute(value, axis, [(source, source + steps) for source in range(first, last)])


def with_halo(x, sides, width):
    for axis, dim in sides:
        count, length = (lax.axis_size(axis), x.shape[dim])
        up = [(i, (i + 1) % count) for i in range(count - 1)]
        down = [(j, i) for i, j in up]
        last = lax.slice_in_dim(x, length - width, length, axis=dim)
        first = lax.slice_in_dim(x, 0, width, axis=dim)
        before = lax.ppermute(last, axis, up)
        after = lax.ppermute(first, axis, down)
        x = jnp.concatenate([before, x, after], axis=dim)
    return x


def left_mul(matrix, field):
    return jnp.einsum("ij,...jk->...ik", matrix, field, precision=lax.Precision.HIGHEST)


def right_mul(field, matrix):
    return jnp.einsum("...ij,jk->...ik", field, matrix, precision=lax.Precision.HIGHEST)


def transform(field, operator_set):
    a_real, a_imag, b_real, b_imag = operator_set
    f_real, f_imag = field
    u_real = left_mul(a_real, f_real) - left_mul(a_imag, f_imag)
    u_imag = left_mul(a_real, f_imag) + left_mul(a_imag, f_real)
    return (
        right_mul(u_real, b_real) - right_mul(u_imag, b_imag),
        right_mul(u_real, b_imag) + right_mul(u_imag, b_real),
    )


def product(first, second):
    return (
        first[0] * second[0] - first[1] * second[1],
        first[0] * second[1] + first[1] * second[0],
    )


def times_conj(first, second):
    return (
        first[0] * second[0] + first[1] * second[1],
        first[1] * second[0] - first[0] * second[1],
    )


def operators(extent):
    counter = jnp.arange(extent, dtype=jnp.int32)
    phase = counter[:, None] * counter[None, :] % extent
    angles = phase.astype(jnp.float32) * (2.0 * math.pi / extent)
    norming = 1.0 / math.sqrt(extent)
    cosine = jnp.cos(angles) * norming
    sine = jnp.sin(angles) * norming
    freq = jnp.where(counter < extent // 2, counter, counter - extent).astype(jnp.float32) / extent
    turned = -math.pi * prop_strength * freq * freq
    h_real = jnp.cos(turned)
    h_imag = jnp.sin(turned)
    a_real = h_real[:, None] * cosine + h_imag[:, None] * sine
    a_imag = h_imag[:, None] * cosine - h_real[:, None] * sine
    highest = lax.Precision.HIGHEST
    q_real = jnp.dot(cosine, a_real, precision=highest) - jnp.dot(sine, a_imag, precision=highest)
    q_imag = jnp.dot(cosine, a_imag, precision=highest) + jnp.dot(sine, a_real, precision=highest)
    forward = (q_real, q_imag, q_real.T, q_imag.T)
    adjoint = (q_real.T, -q_imag.T, q_real, -q_imag)
    far_out = (cosine, -sine, cosine, -sine)
    far_back = (cosine, sine, cosine, sine)
    return (forward, adjoint, far_out, far_back)


def shards(transmission, probe, intensity, positions, batch):
    extent = probe.shape[1]
    half_probe = extent // 2
    layers = transmission.shape[1]
    strip_rows = transmission.shape[2]
    slots = intensity.shape[0]
    depth_count = lax.axis_size("depth")
    last_depth = depth_count - 1
    depth_at = lax.axis_index("depth")
    tile_at = lax.axis_index("tile")
    forward, adjoint, far_out, far_back = operators(extent)
    top_rows = positions[:, 0] - tile_at * strip_rows + half_probe
    left_cols = positions[:, 1]
    group_size = slots // slots
    rounds = depth_count + slots - 1
    zero = jnp.int32(0)
    window = (2, layers, extent, extent)
    numbers = jnp.arange(slots, dtype=jnp.int32)

    def forward_section(entering, obj_patch):
        wavefront = (entering[:, 0], entering[:, 1])
        inputs_seen = []
        for layer in range(layers):
            inputs_seen.append(jnp.stack(wavefront, 1))
            chi = product((obj_patch[:, 0, layer], obj_patch[:, 1, layer]), wavefront)
            wavefront = transform(chi, forward)
        return (jnp.stack(wavefront, 1), jnp.stack(inputs_seen, 2))

    def far_section(leaving, measured, weights):
        far = transform((leaving[:, 0], leaving[:, 1]), far_out)
        resid = far[0] * far[0] + far[1] * far[1] - measured
        factor = 4.0 * resid * weights[:, None, None]
        return jnp.stack(transform((factor * far[0], factor * far[1]), far_back), 1)

    def backward_section(grad_out, inputs_seen, obj_patch):
        grad_wave = (grad_out[:, 0], grad_out[:, 1])
        pieces = []
        for layer in reversed(range(layers)):
            grad_chi = transform(grad_wave, adjoint)
            seen = (inputs_seen[:, 0, layer], inputs_seen[:, 1, layer])
            local_obj = (obj_patch[:, 0, layer], obj_patch[:, 1, layer])
            pieces.append(jnp.stack(times_conj(grad_chi, seen), 1))
            grad_wave = times_conj(grad_chi, local_obj)
        return (jnp.stack(grad_wave, 1), jnp.stack(pieces[::-1], 2))

    def put_group(holder, chosen, in_turn, value):
        return holder.at[chosen].set(jnp.where(in_turn, value, holder[chosen]))

    strip = transmission
    for turn_at in range(2):
        weights = (batch == turn_at).astype(jnp.float32)
        canvas = with_halo(strip, (("tile", 2),), half_probe)

        def cut_window(number):
            return lax.dynamic_slice(
                canvas, (zero, zero, top_rows[number], left_cols[number]), window
            )

        grouped = jax.vmap(cut_window)(numbers).reshape(
            slots, group_size, 2, layers, extent, extent
        )
        measured_groups = intensity.reshape(slots, group_size, extent, extent)
        weight_groups = weights.reshape(slots, group_size)
        entry = probe[None]
        blank_wave = jnp.zeros((group_size, 2, extent, extent), jnp.float32)
        blank_patch = jnp.zeros((group_size, 2, layers, extent, extent), jnp.float32)
        blank_kept = blank_patch
        stored = jnp.zeros((slots,) + blank_kept.shape, jnp.float32)
        far_grads = jnp.zeros((slots,) + blank_wave.shape, jnp.float32)
        run_leaving = blank_wave
        for turn in range(rounds):
            received = from_behind(run_leaving, "depth", 1) if turn > 0 else blank_wave
            group_at = turn - depth_at
            run_in_turn = (group_at >= 0) & (group_at < slots)
            run_chosen = jnp.clip(group_at, 0, slots - 1)
            run_obj_patch = grouped[run_chosen]
            group_weights = weight_groups[run_chosen]
            working = run_in_turn & (jnp.sum(group_weights) > 0)
            run_entering = jnp.where(depth_at == 0, entry, received)

            def active():
                leaving_now, seen = forward_section(run_entering, run_obj_patch)
                far_now = lax.cond(
                    depth_at == last_depth,
                    lambda: far_section(leaving_now, measured_groups[run_chosen], group_weights),
                    lambda: blank_wave,
                )
                return (leaving_now, seen, far_now)

            def resting():
                return (blank_wave, blank_kept, blank_wave)

            run_leaving, seen_now, far_now = lax.cond(working, active, resting)
            stored = put_group(stored, run_chosen, run_in_turn, seen_now)
            far_grads = put_group(far_grads, run_chosen, run_in_turn, far_now)
        run_grad_patches = jnp.zeros((slots,) + blank_patch.shape, jnp.float32)
        grad_leaving = blank_wave
        for turn in range(rounds):
            received = from_behind(grad_leaving, "depth", -1) if turn > 0 else blank_wave
            group_at = turn - (last_depth - depth_at)
            run_in_turn = (group_at >= 0) & (group_at < slots)
            run_chosen = jnp.clip(group_at, 0, slots - 1)
            run_obj_patch = grouped[run_chosen]
            working = run_in_turn & (jnp.sum(weight_groups[run_chosen]) > 0)
            grad_in = jnp.where(depth_at == last_depth, far_grads[run_chosen], received)
            kept = stored[run_chosen]

            def active():
                return backward_section(grad_in, kept, run_obj_patch)

            def resting():
                return (blank_wave, blank_patch)

            grad_leaving, patch_grad = lax.cond(working, active, resting)
            run_grad_patches = put_group(run_grad_patches, run_chosen, run_in_turn, patch_grad)
        grad_patches = run_grad_patches.reshape(slots, 2, layers, extent, extent)

        def place(number, canvas_sum):
            start = (zero, zero, top_rows[number], left_cols[number])
            region = lax.dynamic_slice(canvas_sum, start, window) + grad_patches[number]
            return lax.dynamic_update_slice(canvas_sum, region, start)

        grad_canvas = lax.fori_loop(0, slots, place, jnp.zeros(canvas.shape, jnp.float32))
        from_above = from_behind(grad_canvas[:, :, strip_rows + half_probe :], "tile", 1)
        from_below = from_behind(grad_canvas[:, :, :half_probe], "tile", -1)
        inner = grad_canvas[:, :, half_probe : half_probe + strip_rows]
        inner = inner.at[:, :, :half_probe].add(from_above)
        inner = inner.at[:, :, strip_rows - half_probe :].add(from_below)
        strip = strip - step_rate * inner
    return strip


def solution(mesh):
    return jax.shard_map(
        shards,
        mesh=mesh,
        in_specs=(
            P(None, "depth", "tile", None),
            P(),
            P("tile", None, None),
            P("tile", None),
            P("tile"),
        ),
        out_specs=P(None, "depth", "tile", None),
        check_vma=False,
    )
```

profile of v0, /device:TPU:3, one launch (start us, length us, event | category | flops | bytes accessed | tf_op | source)
XLA Modules:
  0.0 867.2 jit_solution(8243223361431861089)
XLA Ops:
  27.2 4.5 collective-permute-done.1
  31.7 4.2 pad_maximum_fusion.46
  37.4 9.4 %while.64 = (s32[]{:T(128)}, f32[2,2,512,512]{3,2,1,0:T(8,128)}, s32[2,4]{1,0:T(2,128)S(1)}, f32[2,2,2,256,256]{4,3,2,1,0:T(8,128)}, s32[]{:T(128)}) while((s32[]{:T(128)}, f32[2,2,512,512]{3,2,1,0:T(8,128)}, s32[2,4]{1,0:T(2,128)S(1)}, f32[2,2,2,256,256]{4,3,2,1,0:T(8,128)}, s32[]{:T(128)}) %tuple.816), condition=%wide.while_cond.34, body=%wide.while_body.34.sunk | while | flops 2 | bytes 2098801 | solution.py:141
  38.1 4.0 bitcast_dynamic-update-slice_fusion.12
  42.8 4.0 bitcast_dynamic-update-slice_fusion.12
  46.8 22.3 %conditional.30 = (f32[1,2,256,256]{3,2,1,0:T(8,128)}, f32[1,2,256,256]{3,2,1,0:T(8,128)}, f32[1,2,2,256,256]{4,3,2,1,0:T(8,128)}) conditional(s32[]{:T(128)} %convert_element_type.471, () %tuple.466, (f32[2,2,2,256,256]{4,3,2,1,0:T(8,128)}, s32[]{:T(128)}, f32[1,2,256,256]{3,2,1,0:T(8,128)S(1)}, f32[256,256]{1,0:T(8,128)S(1)}, ...), branch_computations={%region_2.3_spmd, %region_3.6_spmd} | conditional | flops 6445400064 | bytes 42467680 | solution.py:179
  76.7 4.8 collective-permute-done.2
  81.5 24.5 %conditional.31 = (f32[1,2,256,256]{3,2,1,0:T(8,128)}, f32[1,2,256,256]{3,2,1,0:T(8,128)}, f32[1,2,2,256,256]{4,3,2,1,0:T(8,128)}) conditional(s32[]{:T(128)} %convert_element_type.474, () %tuple.468, (f32[2,2,2,256,256]{4,3,2,1,0:T(8,128)}, s32[]{:T(128)}, pred[1,2,256,256]{3,2,1,0:T(8,128)(4,1)S(1)}, f32[1,2,256,256]{3,2,1,0:T(8,128)S(1)}, ...), branch_computations={%region_7.8_spmd, %region_8.11_spmd} | conditional | flops 6445531136 | bytes 48366004 | solution.py:179
  106.0 3.9 collective-permute-start.3
  116.2 5.7 collective-permute-done.3
  121.8 10.5 %conditional.32 = (f32[1,2,256,256]{3,2,1,0:T(8,128)}, f32[1,2,256,256]{3,2,1,0:T(8,128)}, f32[1,2,2,256,256]{4,3,2,1,0:T(8,128)}) conditional(s32[]{:T(128)} %convert_element_type.475, () %tuple.470, (f32[2,2,2,256,256]{4,3,2,1,0:T(8,128)}, s32[]{:T(128)}, pred[1,2,256,256]{3,2,1,0:T(8,128)(4,1)S(1)}, f32[1,2,256,256]{3,2,1,0:T(8,128)S(1)}, ...), branch_computations={%region_12.13_spmd, %region_13.16_spmd} | conditional | flops 6445531136 | bytes 48366004 | solution.py:179
  132.3 17.9 %collective-permute-start.4 = (f32[1,2,256,256]{3,2,1,0:T(8,128)}, f32[1,2,256,256]{3,2,1,0:T(8,128)S(1)}, u32[]{:S(2)}, u32[]{:S(2)}) collective-permute-start(f32[1,2,256,256]{3,2,1,0:T(8,128)} %get-tuple-element.3542), channel_id=1, source_target_pairs={{0,8},{8,16},{16,24},{1,9},{9,17},{17,25},{2,10},{10,18},{18,26},{... | collective-permute-start | bytes 1572872 | tf_op jit(solution)/shard_map/ppermute | solution.py:15
  156.7 10.7 %conditional.33 = (f32[1,2,256,256]{3,2,1,0:T(8,128)}, f32[1,2,256,256]{3,2,1,0:T(8,128)}, f32[1,2,2,256,256]{4,3,2,1,0:T(8,128)}) conditional(s32[]{:T(128)} %convert_element_type.476, () %tuple.472, (f32[2,2,2,256,256]{4,3,2,1,0:T(8,128)}, s32[]{:T(128)}, pred[1,2,256,256]{3,2,1,0:T(8,128)(4,1)S(1)}, f32[1,2,256,256]{3,2,1,0:T(8,128)S(1)}, ...), branch_computations={%region_17.18_spmd, %region_18.21_spmd} | conditional | flops 6445531136 | bytes 48366004 | solution.py:179
  167.4 7.3 collective-permute-start.5
  180.5 4.9 collective-permute-done.5
  185.4 10.0 %conditional.34 = (f32[1,2,256,256]{3,2,1,0:T(8,128)}, f32[1,2,2,256,256]{4,3,2,1,0:T(8,128)}) conditional(s32[]{:T(128)} %convert_element_type.477, () %tuple.474, (pred[1,2,256,256]{3,2,1,0:T(8,128)(4,1)S(1)}, f32[1,2,256,256]{3,2,1,0:T(8,128)S(1)}, f32[1,2,256,256]{3,2,1,0:T(8,128)S(1)}, f32[2,2,2,256,256]{4,3,2,1,0:T(8,128)}, s32[]{:T(128)}, ...), branch_computations={%region_22.23_spmd, %region_23.26_spmd} | conditional | flops 6445531136 | bytes 49938932 | solution.py:179
  204.1 18.3 %collective-permute-done.6 = f32[1,2,256,256]{3,2,1,0:T(8,128)} collective-permute-done((f32[1,2,256,256]{3,2,1,0:T(8,128)}, f32[1,2,256,256]{3,2,1,0:T(8,128)}, u32[]{:S(2)}, u32[]{:S(2)}) %collective-permute-start.6) | collective-permute-done | bytes 524320 | tf_op jit(solution)/shard_map/ppermute | solution.py:15
  228.7 25.6 %collective-permute-done.7 = f32[1,2,256,256]{3,2,1,0:T(8,128)} collective-permute-done((f32[1,2,256,256]{3,2,1,0:T(8,128)}, f32[1,2,256,256]{3,2,1,0:T(8,128)}, u32[]{:S(2)}, u32[]{:S(2)}) %collective-permute-start.7) | collective-permute-done | bytes 524320 | tf_op jit(solution)/shard_map/ppermute | solution.py:15
  261.3 71.7 %collective-permute-done.8 = f32[1,2,256,256]{3,2,1,0:T(8,128)S(1)} collective-permute-done((f32[1,2,256,256]{3,2,1,0:T(8,128)}, f32[1,2,256,256]{3,2,1,0:T(8,128)S(1)}, u32[]{:S(2)}, u32[]{:S(2)}) %collective-permute-start.8) | collective-permute-done | bytes 524320 | tf_op jit(solution)/shard_map/ppermute | solution.py:15
  333.0 17.0 %conditional.38 = (f32[1,2,256,256]{3,2,1,0:T(8,128)}, f32[1,2,2,256,256]{4,3,2,1,0:T(8,128)}) conditional(s32[]{:T(128)} %convert_element_type.480, () %tuple.481, (f32[2,1,2,256,256]{4,3,2,1,0:T(8,128)S(1)}, s32[]{:T(128)}, pred[1,2,256,256]{3,2,1,0:T(8,128)(4,1)S(1)}, f32[1,2,256,256]{3,2,1,0:T(8,128)S(1)}, f32[256,256]{0,1:T(8,128)S(1)}, ...), branch_computations={%region_40.41_spmd, %region_41.42_spmd} | conditional | flops 3224109056 | bytes 41287816 | solution.py:200
  360.5 12.5 %conditional.39 = (f32[1,2,2,256,256]{4,3,2,1,0:T(8,128)}) conditional(s32[]{:T(128)} %convert_element_type.481, () %tuple.483, (f32[2,1,2,256,256]{4,3,2,1,0:T(8,128)S(1)}, s32[]{:T(128)}, pred[1,2,256,256]{3,2,1,0:T(8,128)(4,1)S(1)}, f32[1,2,256,256]{3,2,1,0:T(8,128)S(1)}, f32[256,256]{0,1:T(8,128)S(1)}, /*index=5*/f32[256,256]{0,1:T(8,128)S(1)}, ...), branch_computations={%region_43.44_spmd, %region_44.45_spmd} | conditional | flops 3223584768 | bytes 37093440 | solution.py:200
  378.9 38.1 %while.62 = (s32[]{:T(128)}, f32[2,2,512,512]{3,2,1,0:T(8,128)}, s32[2]{0:T(128)S(1)}, s32[2]{0:T(128)S(1)}, f32[2,2,2,256,256]{4,3,2,1,0:T(8,128)}, /*index=5*/s32[]{:T(128)}, s32[]{:T(128)}, s32[]{:T(128)}) while((s32[]{:T(128)}, f32[2,2,512,512]{3,2,1,0:T(8,128)}, s32[2]{0:T(128)S(1)}, s32[2]{0:T(128)S(1)}, ...), condition=%wide.region_46.47_spmd, body=%wide.region_45.46_spmd.sunk | while | flops 262152 | bytes 5243073 | solution.py:209
  386.1 12.2 %dynamic_update_slice.16 = f32[2,2,512,512]{3,2,1,0:T(8,128)} dynamic-update-slice(f32[2,2,512,512]{3,2,1,0:T(8,128)} %get-tuple-element.4878, f32[2,2,256,256]{3,2,1,0:T(8,128)S(1)} %bitcast_add_fusion.4, s32[]{:T(128)} %constant.1150.clone.1..sunk, s32[]{:T(128)} %constant.1150.clone.1..sunk, s32[]{:T(128)S(6)} %select_n.1097, s32[]{:T(128)S(6)} %select_n.1098) | dynamic-update-slice | bytes 2097156 | tf_op jit(solution)/shard_map/while/body/eval_jaxpr/dynamic_update_slice | solution.py:207
  405.5 11.5 %dynamic_update_slice.16 = f32[2,2,512,512]{3,2,1,0:T(8,128)} dynamic-update-slice(f32[2,2,512,512]{3,2,1,0:T(8,128)} %get-tuple-element.4878, f32[2,2,256,256]{3,2,1,0:T(8,128)S(1)} %bitcast_add_fusion.4, s32[]{:T(128)} %constant.1150.clone.1..sunk, s32[]{:T(128)} %constant.1150.clone.1..sunk, s32[]{:T(128)S(6)} %select_n.1097, s32[]{:T(128)S(6)} %select_n.1098) | dynamic-update-slice | bytes 2097156 | tf_op jit(solution)/shard_map/while/body/eval_jaxpr/dynamic_update_slice | solution.py:207
  423.8 17.5 %collective-permute-done.10 = f32[2,2,128,512]{3,2,1,0:T(8,128)S(1)} collective-permute-done((f32[2,2,128,512]{3,2,1,0:T(8,128)S(1)}, f32[2,2,128,512]{3,2,1,0:T(8,128)S(1)}, u32[]{:S(2)}, u32[]{:S(2)}) %collective-permute-start.10) | collective-permute-done | bytes 1048608 | tf_op jit(solution)/shard_map/ppermute | solution.py:15
  446.3 4.3 collective-permute-start.12
  456.1 15.7 %collective-permute-done.12 = f32[2,2,128,512]{3,2,1,0:T(8,128)} collective-permute-done((f32[2,2,128,512]{3,2,1,0:T(8,128)}, f32[2,2,128,512]{3,2,1,0:T(8,128)}, u32[]{:S(2)}, u32[]{:S(2)}) %collective-permute-start.12) | collective-permute-done | bytes 1048608 | tf_op jit(solution)/shard_map/ppermute | solution.py:25
  471.8 4.7 pad_maximum_fusion.47
  478.0 9.2 %while.65 = (s32[]{:T(128)}, f32[2,2,512,512]{3,2,1,0:T(8,128)}, s32[2,4]{1,0:T(2,128)S(1)}, f32[2,2,2,256,256]{4,3,2,1,0:T(8,128)}, s32[]{:T(128)}) while((s32[]{:T(128)}, f32[2,2,512,512]{3,2,1,0:T(8,128)}, s32[2,4]{1,0:T(2,128)S(1)}, f32[2,2,2,256,256]{4,3,2,1,0:T(8,128)}, s32[]{:T(128)}) %tuple.1074), condition=%wide.while_cond.35, body=%wide.while_body.35.sunk | while | flops 2 | bytes 2098801 | solution.py:141
  478.6 4.0 bitcast_dynamic-update-slice_fusion.13
  483.2 4.0 bitcast_dynamic-update-slice_fusion.13
  487.2 11.0 %conditional.40 = (f32[1,2,256,256]{3,2,1,0:T(8,128)}, f32[1,2,256,256]{3,2,1,0:T(8,128)}, f32[1,2,2,256,256]{4,3,2,1,0:T(8,128)}) conditional(s32[]{:T(128)} %convert_element_type.484, () %tuple.487, (f32[2,2,2,256,256]{4,3,2,1,0:T(8,128)}, s32[]{:T(128)}, f32[1,2,256,256]{3,2,1,0:T(8,128)S(1)}, f32[256,256]{1,0:T(8,128)S(1)}, ...), branch_computations={%region_47.48_spmd, %region_48.51_spmd} | conditional | flops 6445400064 | bytes 42467680 | solution.py:179
  508.9 10.5 %conditional.41 = (f32[1,2,256,256]{3,2,1,0:T(8,128)}, f32[1,2,256,256]{3,2,1,0:T(8,128)}, f32[1,2,2,256,256]{4,3,2,1,0:T(8,128)}) conditional(s32[]{:T(128)} %convert_element_type.485, () %tuple.489, (f32[2,2,2,256,256]{4,3,2,1,0:T(8,128)}, s32[]{:T(128)}, pred[1,2,256,256]{3,2,1,0:T(8,128)(4,1)S(1)}, f32[1,2,256,256]{3,2,1,0:T(8,128)S(1)}, ...), branch_computations={%region_51.52_spmd, %region_52.55_spmd} | conditional | flops 6445531136 | bytes 48366004 | solution.py:179
  519.4 4.2 collective-permute-start.15
  530.4 10.7 %conditional.42 = (f32[1,2,256,256]{3,2,1,0:T(8,128)}, f32[1,2,256,256]{3,2,1,0:T(8,128)}, f32[1,2,2,256,256]{4,3,2,1,0:T(8,128)}) conditional(s32[]{:T(128)} %convert_element_type.486, () %tuple.491, (f32[2,2,2,256,256]{4,3,2,1,0:T(8,128)}, s32[]{:T(128)}, pred[1,2,256,256]{3,2,1,0:T(8,128)(4,1)S(1)}, f32[1,2,256,256]{3,2,1,0:T(8,128)S(1)}, ...), branch_computations={%region_55.56_spmd, %region_56.59_spmd} | conditional | flops 6445531136 | bytes 48366004 | solution.py:179
  541.1 4.0 collective-permute-start.16
  551.6 10.7 %conditional.43 = (f32[1,2,256,256]{3,2,1,0:T(8,128)}, f32[1,2,256,256]{3,2,1,0:T(8,128)}, f32[1,2,2,256,256]{4,3,2,1,0:T(8,128)}) conditional(s32[]{:T(128)} %convert_element_type.487, () %tuple.493, (f32[2,2,2,256,256]{4,3,2,1,0:T(8,128)}, s32[]{:T(128)}, pred[1,2,256,256]{3,2,1,0:T(8,128)(4,1)S(1)}, f32[1,2,256,256]{3,2,1,0:T(8,128)S(1)}, ...), branch_computations={%region_59.60_spmd, %region_60.63_spmd} | conditional | flops 6445531136 | bytes 48366004 | solution.py:179
  562.2 4.5 collective-permute-start.17
  573.2 9.7 %conditional.44 = (f32[1,2,256,256]{3,2,1,0:T(8,128)}, f32[1,2,2,256,256]{4,3,2,1,0:T(8,128)}) conditional(s32[]{:T(128)} %convert_element_type.488, () %tuple.495, (pred[1,2,256,256]{3,2,1,0:T(8,128)(4,1)S(1)}, f32[1,2,256,256]{3,2,1,0:T(8,128)S(1)}, f32[1,2,256,256]{3,2,1,0:T(8,128)S(1)}, f32[2,2,2,256,256]{4,3,2,1,0:T(8,128)}, s32[]{:T(128)}, ...), branch_computations={%region_63.64_spmd, %region_64.67_spmd} | conditional | flops 6445531136 | bytes 50987508 | solution.py:179
  588.9 8.5 collective-permute-done.18
  603.0 6.8 collective-permute-done.19
  614.8 6.7 collective-permute-done.20
  638.9 38.2 %while.63 = (s32[]{:T(128)}, f32[2,2,512,512]{3,2,1,0:T(8,128)}, s32[2]{0:T(128)S(1)}, s32[2]{0:T(128)S(1)}, f32[2,2,2,256,256]{4,3,2,1,0:T(8,128)}, /*index=5*/s32[]{:T(128)}, s32[]{:T(128)}, s32[]{:T(128)}) while((s32[]{:T(128)}, f32[2,2,512,512]{3,2,1,0:T(8,128)}, s32[2]{0:T(128)S(1)}, s32[2]{0:T(128)S(1)}, ...), condition=%wide.region_78.79_spmd, body=%wide.region_77.78_spmd.sunk | while | flops 262152 | bytes 5243073 | solution.py:209
  646.0 12.3 %dynamic_update_slice.17 = f32[2,2,512,512]{3,2,1,0:T(8,128)} dynamic-update-slice(f32[2,2,512,512]{3,2,1,0:T(8,128)} %get-tuple-element.4963, f32[2,2,256,256]{3,2,1,0:T(8,128)S(1)} %bitcast_add_fusion.5, s32[]{:T(128)} %constant.1150.clone.1..sunk.1, s32[]{:T(128)} %constant.1150.clone.1..sunk.1, s32[]{:T(128)S(6)} %select_n.1099, s32[]{:T(128)S(6)} %select_n.1100) | dynamic-update-slice | bytes 2097156 | tf_op jit(solution)/shard_map/while/body/eval_jaxpr/dynamic_update_slice | solution.py:207
  665.5 11.6 %dynamic_update_slice.17 = f32[2,2,512,512]{3,2,1,0:T(8,128)} dynamic-update-slice(f32[2,2,512,512]{3,2,1,0:T(8,128)} %get-tuple-element.4963, f32[2,2,256,256]{3,2,1,0:T(8,128)S(1)} %bitcast_add_fusion.5, s32[]{:T(128)} %constant.1150.clone.1..sunk.1, s32[]{:T(128)} %constant.1150.clone.1..sunk.1, s32[]{:T(128)S(6)} %select_n.1099, s32[]{:T(128)S(6)} %select_n.1100) | dynamic-update-slice | bytes 2097156 | tf_op jit(solution)/shard_map/while/body/eval_jaxpr/dynamic_update_slice | solution.py:207
  679.0 168.6 %collective-permute-start.22 = (f32[2,2,128,512]{3,2,1,0:T(8,128)S(1)}, f32[2,2,128,512]{3,2,1,0:T(8,128)S(1)}, u32[]{:S(2)}, u32[]{:S(2)}) collective-permute-start(f32[2,2,128,512]{3,2,1,0:T(8,128)S(1)} %get-tuple-element.4641), channel_id=1, source_target_pairs={{0,1},{1,2},{2,3},{3,4},{4,5},{5,6},{6,7},{8,9},{9,10},{10,11},{11... | collective-permute-start | bytes 3145736 | tf_op jit(solution)/shard_map/ppermute | solution.py:15
  849.7 9.6 %collective-permute-done.22 = f32[2,2,128,512]{3,2,1,0:T(8,128)S(1)} collective-permute-done((f32[2,2,128,512]{3,2,1,0:T(8,128)S(1)}, f32[2,2,128,512]{3,2,1,0:T(8,128)S(1)}, u32[]{:S(2)}, u32[]{:S(2)}) %collective-permute-start.22) | collective-permute-done | bytes 1048608 | tf_op jit(solution)/shard_map/ppermute | solution.py:15
  859.5 5.1 collective-permute-done.23
  (403 shorter events, 278.0 us)
Async XLA Ops:
  0.0 11.7 %copy-start.114 = (s32[2]{0:T(128)S(1)}, s32[2]{0:T(128)}, u32[]{:S(2)}) copy-start(s32[2]{0:T(128)} %param.141) | copy-start | bytes 28
  3.1 24.1 %collective-permute-start = (f32[2,2,128,512]{3,2,1,0:T(8,128)}, f32[2,2,128,512]{3,2,1,0:T(8,128)}, u32[]{:S(2)}, u32[]{:S(2)}) collective-permute-start(f32[2,2,128,512]{3,2,1,0:T(8,128)} %get-tuple-element.4646), channel_id=1, source_target_pairs={{0,1},{1,2},{2,3},{3,4},{4,5},{5,6},{6,7},{8,9},{9,10},{10,11},{11... | collective-permute-start | bytes 3145736 | tf_op jit(solution)/shard_map/ppermute | solution.py:25
  6.8 24.9 %collective-permute-start.1 = (f32[2,2,128,512]{3,2,1,0:T(8,128)}, f32[2,2,128,512]{3,2,1,0:T(8,128)}, u32[]{:S(2)}, u32[]{:S(2)}) collective-permute-start(f32[2,2,128,512]{3,2,1,0:T(8,128)} %get-tuple-element.4647), channel_id=1, source_target_pairs={{1,0},{2,1},{3,2},{4,3},{5,4},{6,5},{7,6},{9,8},{10,9},{11,10},{12... | collective-permute-start | bytes 3145736 | tf_op jit(solution)/shard_map/ppermute | solution.py:26
  13.2 8.2 copy-start.113
  13.2 9.0 %copy-start.112 = (s32[5]{0:T(128)S(1)}, s32[5]{0:T(128)}, u32[]{:S(2)}) copy-start(s32[5]{0:T(128)} %constant.1171.clone.1) | copy-start | bytes 64
  24.6 7.1 copy-start.39
  26.1 20.7 %copy-start.44 = (f32[1,2,256,256]{3,2,1,0:T(8,128)}, f32[1,2,256,256]{3,2,1,0:T(8,128)S(1)}, u32[]{:S(2)}) copy-start(f32[1,2,256,256]{3,2,1,0:T(8,128)S(1)} %select_bitcast_fusion) | copy-start | bytes 1572868
  37.4 9.4 %copy-start.41 = (f32[2,256,256]{2,1,0:T(8,128)S(1)}, f32[2,256,256]{2,1,0:T(8,128)}, u32[]{:S(2)}) copy-start(f32[2,256,256]{2,1,0:T(8,128)} %param.139) | copy-start | bytes 1572868
  69.2 12.3 %collective-permute-start.2 = (f32[1,2,256,256]{3,2,1,0:T(8,128)}, f32[1,2,256,256]{3,2,1,0:T(8,128)S(1)}, u32[]{:S(2)}, u32[]{:S(2)}) collective-permute-start(f32[1,2,256,256]{3,2,1,0:T(8,128)} %get-tuple-element.3538), channel_id=1, source_target_pairs={{0,8},{8,16},{16,24},{1,9},{9,17},{17,25},{2,10},{10,18},{18,26},{... | collective-permute-start | bytes 1572872 | tf_op jit(solution)/shard_map/ppermute | solution.py:15
  81.5 104.0 %copy-start.46 = (pred[1,2,256,256]{3,2,1,0:T(8,128)(4,1)}, pred[1,2,256,256]{3,2,1,0:T(8,128)(4,1)S(1)}, u32[]{:S(2)}) copy-start(pred[1,2,256,256]{3,2,1,0:T(8,128)(4,1)S(1)} %select_n.884) | copy-start | bytes 393220
  106.0 6.7 copy-start.13
  106.0 15.8 %collective-permute-start.3 = (f32[1,2,256,256]{3,2,1,0:T(8,128)}, f32[1,2,256,256]{3,2,1,0:T(8,128)S(1)}, u32[]{:S(2)}, u32[]{:S(2)}) collective-permute-start(f32[1,2,256,256]{3,2,1,0:T(8,128)} %get-tuple-element.3540), channel_id=1, source_target_pairs={{0,8},{8,16},{16,24},{1,9},{9,17},{17,25},{2,10},{10,18},{18,26},{... | collective-permute-start | bytes 1572872 | tf_op jit(solution)/shard_map/ppermute | solution.py:15
  115.0 6.8 copy-start.14
  132.3 20.5 %copy-start.15 = (f32[2,1,2,2,256,256]{5,4,3,2,1,0:T(8,128)S(1)}, f32[2,1,2,2,256,256]{5,4,3,2,1,0:T(8,128)}, u32[]{:S(2)}) copy-start(f32[2,1,2,2,256,256]{5,4,3,2,1,0:T(8,128)} %copy-done.14) | copy-start | bytes 6291460
  132.3 24.3 %collective-permute-start.4 = (f32[1,2,256,256]{3,2,1,0:T(8,128)}, f32[1,2,256,256]{3,2,1,0:T(8,128)S(1)}, u32[]{:S(2)}, u32[]{:S(2)}) collective-permute-start(f32[1,2,256,256]{3,2,1,0:T(8,128)} %get-tuple-element.3542), channel_id=1, source_target_pairs={{0,8},{8,16},{16,24},{1,9},{9,17},{17,25},{2,10},{10,18},{18,26},{... | collective-permute-start | bytes 1572872 | tf_op jit(solution)/shard_map/ppermute | solution.py:15
  167.4 10.0 %copy-start.17 = (f32[2,1,2,2,256,256]{5,4,3,2,1,0:T(8,128)S(1)}, f32[2,1,2,2,256,256]{5,4,3,2,1,0:T(8,128)}, u32[]{:S(2)}) copy-start(f32[2,1,2,2,256,256]{5,4,3,2,1,0:T(8,128)} %copy-done.16) | copy-start | bytes 6291460
  167.4 18.0 %collective-permute-start.5 = (f32[1,2,256,256]{3,2,1,0:T(8,128)}, f32[1,2,256,256]{3,2,1,0:T(8,128)S(1)}, u32[]{:S(2)}, u32[]{:S(2)}) collective-permute-start(f32[1,2,256,256]{3,2,1,0:T(8,128)} %get-tuple-element.3544), channel_id=1, source_target_pairs={{0,8},{8,16},{16,24},{1,9},{9,17},{17,25},{2,10},{10,18},{18,26},{... | collective-permute-start | bytes 1572872 | tf_op jit(solution)/shard_map/ppermute | solution.py:15
  179.3 6.2 copy-start.18
  202.2 20.2 %collective-permute-start.6 = (f32[1,2,256,256]{3,2,1,0:T(8,128)}, f32[1,2,256,256]{3,2,1,0:T(8,128)}, u32[]{:S(2)}, u32[]{:S(2)}) collective-permute-start(f32[1,2,256,256]{3,2,1,0:T(8,128)} %get-tuple-element.3552), channel_id=1, source_target_pairs={{8,0},{16,8},{24,16},{9,1},{17,9},{25,17},{10,2},{18,10},{26,18},{... | collective-permute-start | bytes 1572872 | tf_op jit(solution)/shard_map/ppermute | solution.py:15
  224.6 29.7 %collective-permute-start.7 = (f32[1,2,256,256]{3,2,1,0:T(8,128)}, f32[1,2,256,256]{3,2,1,0:T(8,128)}, u32[]{:S(2)}, u32[]{:S(2)}) collective-permute-start(f32[1,2,256,256]{3,2,1,0:T(8,128)} %get-tuple-element.3554), channel_id=1, source_target_pairs={{8,0},{16,8},{24,16},{9,1},{17,9},{25,17},{10,2},{18,10},{26,18},{... | collective-permute-start | bytes 1572872 | tf_op jit(solution)/shard_map/ppermute | solution.py:15
  228.7 25.6 %copy-start.34 = (f32[2,1,2,2,256,256]{5,4,3,2,1,0:T(8,128)}, f32[2,1,2,2,256,256]{5,4,3,2,1,0:T(8,128)S(1)}, u32[]{:S(2)}) copy-start(f32[2,1,2,2,256,256]{5,4,3,2,1,0:T(8,128)S(1)} %bitcast_dynamic-update-slice_fusion.6) | copy-start | bytes 6291460
  256.5 76.5 %collective-permute-start.8 = (f32[1,2,256,256]{3,2,1,0:T(8,128)}, f32[1,2,256,256]{3,2,1,0:T(8,128)S(1)}, u32[]{:S(2)}, u32[]{:S(2)}) collective-permute-start(f32[1,2,256,256]{3,2,1,0:T(8,128)} %get-tuple-element.3556), channel_id=1, source_target_pairs={{8,0},{16,8},{24,16},{9,1},{17,9},{25,17},{10,2},{18,10},{26,18},{... | collective-permute-start | bytes 1572872 | tf_op jit(solution)/shard_map/ppermute | solution.py:15
  260.1 72.9 %copy-start.36 = (f32[2,1,2,2,256,256]{5,4,3,2,1,0:T(8,128)}, f32[2,1,2,2,256,256]{5,4,3,2,1,0:T(8,128)S(1)}, u32[]{:S(2)}) copy-start(f32[2,1,2,2,256,256]{5,4,3,2,1,0:T(8,128)S(1)} %fusion.217) | copy-start | bytes 6291460
  350.0 10.5 %collective-permute-start.9 = (f32[1,2,256,256]{3,2,1,0:T(8,128)}, f32[1,2,256,256]{3,2,1,0:T(8,128)S(1)}, u32[]{:S(2)}, u32[]{:S(2)}) collective-permute-start(f32[1,2,256,256]{3,2,1,0:T(8,128)} %get-tuple-element.3558), channel_id=1, source_target_pairs={{8,0},{16,8},{24,16},{9,1},{17,9},{25,17},{10,2},{18,10},{26,18},{... | collective-permute-start | bytes 1572872 | tf_op jit(solution)/shard_map/ppermute | solution.py:15
  417.1 6.6 copy-start.25
  419.0 22.3 %collective-permute-start.10 = (f32[2,2,128,512]{3,2,1,0:T(8,128)S(1)}, f32[2,2,128,512]{3,2,1,0:T(8,128)S(1)}, u32[]{:S(2)}, u32[]{:S(2)}) collective-permute-start(f32[2,2,128,512]{3,2,1,0:T(8,128)S(1)} %get-tuple-element.4643), channel_id=1, source_target_pairs={{0,1},{1,2},{2,3},{3,4},{4,5},{5,6},{6,7},{8,9},{9,10},{10,11},{11... | collective-permute-start | bytes 3145736 | tf_op jit(solution)/shard_map/ppermute | solution.py:15
  421.0 22.8 %collective-permute-start.11 = (f32[2,2,128,512]{3,2,1,0:T(8,128)S(1)}, f32[2,2,128,512]{3,2,1,0:T(8,128)S(1)}, u32[]{:S(2)}, u32[]{:S(2)}) collective-permute-start(f32[2,2,128,512]{3,2,1,0:T(8,128)S(1)} %get-tuple-element.4642), channel_id=1, source_target_pairs={{1,0},{2,1},{3,2},{4,3},{5,4},{6,5},{7,6},{9,8},{10,9},{11,10},{12... | collective-permute-start | bytes 3145736 | tf_op jit(solution)/shard_map/ppermute | solution.py:15
  446.3 25.5 %collective-permute-start.12 = (f32[2,2,128,512]{3,2,1,0:T(8,128)}, f32[2,2,128,512]{3,2,1,0:T(8,128)}, u32[]{:S(2)}, u32[]{:S(2)}) collective-permute-start(f32[2,2,128,512]{3,2,1,0:T(8,128)} %get-tuple-element.4644), channel_id=1, source_target_pairs={{0,1},{1,2},{2,3},{3,4},{4,5},{5,6},{6,7},{8,9},{9,10},{10,11},{11... | collective-permute-start | bytes 3145736 | tf_op jit(solution)/shard_map/ppermute | solution.py:25
  450.6 21.2 %collective-permute-start.13 = (f32[2,2,128,512]{3,2,1,0:T(8,128)S(1)}, f32[2,2,128,512]{3,2,1,0:T(8,128)}, u32[]{:S(2)}, u32[]{:S(2)}) collective-permute-start(f32[2,2,128,512]{3,2,1,0:T(8,128)S(1)} %get-tuple-element.4645), channel_id=1, source_target_pairs={{1,0},{2,1},{3,2},{4,3},{5,4},{6,5},{7,6},{9,8},{10,9},{11,10},{12... | collective-permute-start | bytes 3145736 | tf_op jit(solution)/shard_map/ppermute | solution.py:26
  478.0 9.2 %copy-start.42 = (f32[2,256,256]{2,1,0:T(8,128)S(1)}, f32[2,256,256]{2,1,0:T(8,128)}, u32[]{:S(2)}) copy-start(f32[2,256,256]{2,1,0:T(8,128)} %param.139) | copy-start | bytes 1572868
  478.0 9.2 %copy-start.45 = (f32[1,2,256,256]{3,2,1,0:T(8,128)S(1)}, f32[1,2,256,256]{3,2,1,0:T(8,128)}, u32[]{:S(2)}) copy-start(f32[1,2,256,256]{3,2,1,0:T(8,128)} %copy-done.44) | copy-start | bytes 1572868
  498.2 10.7 %collective-permute-start.14 = (f32[1,2,256,256]{3,2,1,0:T(8,128)}, f32[1,2,256,256]{3,2,1,0:T(8,128)S(1)}, u32[]{:S(2)}, u32[]{:S(2)}) collective-permute-start(f32[1,2,256,256]{3,2,1,0:T(8,128)} %get-tuple-element.3561), channel_id=1, source_target_pairs={{0,8},{8,16},{16,24},{1,9},{9,17},{17,25},{2,10},{10,18},{18,26},{... | collective-permute-start | bytes 1572872 | tf_op jit(solution)/shard_map/ppermute | solution.py:15
  502.4 6.5 copy-start.47
  519.4 7.0 copy-start.1
  519.4 10.6 %collective-permute-start.15 = (f32[1,2,256,256]{3,2,1,0:T(8,128)}, f32[1,2,256,256]{3,2,1,0:T(8,128)S(1)}, u32[]{:S(2)}, u32[]{:S(2)}) collective-permute-start(f32[1,2,256,256]{3,2,1,0:T(8,128)} %get-tuple-element.3563), channel_id=1, source_target_pairs={{0,8},{8,16},{16,24},{1,9},{9,17},{17,25},{2,10},{10,18},{18,26},{... | collective-permute-start | bytes 1572872 | tf_op jit(solution)/shard_map/ppermute | solution.py:15
  541.1 6.6 copy-start.3
  541.1 10.4 %collective-permute-start.16 = (f32[1,2,256,256]{3,2,1,0:T(8,128)}, f32[1,2,256,256]{3,2,1,0:T(8,128)S(1)}, u32[]{:S(2)}, u32[]{:S(2)}) collective-permute-start(f32[1,2,256,256]{3,2,1,0:T(8,128)} %get-tuple-element.3565), channel_id=1, source_target_pairs={{0,8},{8,16},{16,24},{1,9},{9,17},{17,25},{2,10},{10,18},{18,26},{... | collective-permute-start | bytes 1572872 | tf_op jit(solution)/shard_map/ppermute | solution.py:15
  562.2 7.2 copy-start.5
  562.2 10.9 %collective-permute-start.17 = (f32[1,2,256,256]{3,2,1,0:T(8,128)}, f32[1,2,256,256]{3,2,1,0:T(8,128)S(1)}, u32[]{:S(2)}, u32[]{:S(2)}) collective-permute-start(f32[1,2,256,256]{3,2,1,0:T(8,128)} %get-tuple-element.3567), channel_id=1, source_target_pairs={{0,8},{8,16},{16,24},{1,9},{9,17},{17,25},{2,10},{10,18},{18,26},{... | collective-permute-start | bytes 1572872 | tf_op jit(solution)/shard_map/ppermute | solution.py:15
  587.0 10.4 %collective-permute-start.18 = (f32[1,2,256,256]{3,2,1,0:T(8,128)S(1)}, f32[1,2,256,256]{3,2,1,0:T(8,128)}, u32[]{:S(2)}, u32[]{:S(2)}) collective-permute-start(f32[1,2,256,256]{3,2,1,0:T(8,128)S(1)} %get-tuple-element.3575), channel_id=1, source_target_pairs={{8,0},{16,8},{24,16},{9,1},{17,9},{25,17},{10,2},{18,10},{26,18},{... | collective-permute-start | bytes 1572872 | tf_op jit(solution)/shard_map/ppermute | solution.py:15
  598.9 10.9 %collective-permute-start.19 = (f32[1,2,256,256]{3,2,1,0:T(8,128)S(1)}, f32[1,2,256,256]{3,2,1,0:T(8,128)}, u32[]{:S(2)}, u32[]{:S(2)}) collective-permute-start(f32[1,2,256,256]{3,2,1,0:T(8,128)S(1)} %get-tuple-element.3577), channel_id=1, source_target_pairs={{8,0},{16,8},{24,16},{9,1},{17,9},{25,17},{10,2},{18,10},{26,18},{... | collective-permute-start | bytes 1572872 | tf_op jit(solution)/shard_map/ppermute | solution.py:15
  603.0 6.8 copy-start.29
  611.1 10.4 %collective-permute-start.20 = (f32[1,2,256,256]{3,2,1,0:T(8,128)S(1)}, f32[1,2,256,256]{3,2,1,0:T(8,128)S(1)}, u32[]{:S(2)}, u32[]{:S(2)}) collective-permute-start(f32[1,2,256,256]{3,2,1,0:T(8,128)S(1)} %get-tuple-element.3579), channel_id=1, source_target_pairs={{8,0},{16,8},{24,16},{9,1},{17,9},{25,17},{10,2},{18,10},{26,18},{... | collective-permute-start | bytes 1572872 | tf_op jit(solution)/shard_map/ppermute | solution.py:15
  614.7 6.8 copy-start.31
  622.9 10.1 %collective-permute-start.21 = (f32[1,2,256,256]{3,2,1,0:T(8,128)S(1)}, f32[1,2,256,256]{3,2,1,0:T(8,128)S(1)}, u32[]{:S(2)}, u32[]{:S(2)}) collective-permute-start(f32[1,2,256,256]{3,2,1,0:T(8,128)S(1)} %get-tuple-element.3581), channel_id=1, source_target_pairs={{8,0},{16,8},{24,16},{9,1},{17,9},{25,17},{10,2},{18,10},{26,18},{... | collective-permute-start | bytes 1572872 | tf_op jit(solution)/shard_map/ppermute | solution.py:15
  677.1 172.4 %copy-start.24 = (f32[2,2,512,512]{3,2,1,0:T(8,128)S(1)}, f32[2,2,512,512]{3,2,1,0:T(8,128)}, u32[]{:S(2)}) copy-start(f32[2,2,512,512]{3,2,1,0:T(8,128)} %get-tuple-element.3582) | copy-start | bytes 12582916
  679.0 180.4 %collective-permute-start.22 = (f32[2,2,128,512]{3,2,1,0:T(8,128)S(1)}, f32[2,2,128,512]{3,2,1,0:T(8,128)S(1)}, u32[]{:S(2)}, u32[]{:S(2)}) collective-permute-start(f32[2,2,128,512]{3,2,1,0:T(8,128)S(1)} %get-tuple-element.4641), channel_id=1, source_target_pairs={{0,1},{1,2},{2,3},{3,4},{4,5},{5,6},{6,7},{8,9},{9,10},{10,11},{11... | collective-permute-start | bytes 3145736 | tf_op jit(solution)/shard_map/ppermute | solution.py:15
  847.6 17.0 %collective-permute-start.23 = (f32[2,2,128,512]{3,2,1,0:T(8,128)S(1)}, f32[2,2,128,512]{3,2,1,0:T(8,128)S(1)}, u32[]{:S(2)}, u32[]{:S(2)}) collective-permute-start(f32[2,2,128,512]{3,2,1,0:T(8,128)S(1)} %get-tuple-element.4640), channel_id=1, source_target_pairs={{1,0},{2,1},{3,2},{4,3},{5,4},{6,5},{7,6},{9,8},{10,9},{11,10},{12... | collective-permute-start | bytes 3145736 | tf_op jit(solution)/shard_map/ppermute | solution.py:15
  (28 other events, 76.5 us)
where the time goes:
time: 862 us; the launch traced here: 867 us
  starting transfers between devices  242 us (28%)
  waiting for transfers between devices  215 us (25%)
  local copies, waits for them, and re-layouts  159 us (18%)
  loops' own time  94.8 us (11%)
  other arithmetic  90.3 us (10%)
  matrix products  52.8 us (6%)
  between operations  13.8 us (2%)
    ppermute x20, starting transfers between devices, from_behind(): lax.ppermute(value, axis, [(source, source + steps) for source in range(f...  230 us
    ppermute x20, waiting for transfers between devices, from_behind(): lax.ppermute(value, axis, [(source, source + steps) for source in range(f...  193 us
    another operation x10, loops' own time, shards(): run_leaving, seen_now, far_now = lax.cond(working, active, resting)  76.6 us
    scatter x30, other arithmetic, put_group(): return holder.at[chosen].set(jnp.where(in_turn, value, holder[chosen]))  57.8 us
    dynamic_update_slice x4, local copies, waits for them, and re-layouts, place(): return lax.dynamic_update_slice(canvas_sum, region, start)  47.7 us
    another operation x64, local copies, waits for them, and re-layouts  38.6 us
    dot_general x32, matrix products, right_mul(): jnp.einsum('...ij,jk->...ik', field, matrix, precision=lax.Precision.HIGH...  27.8 us
    dynamic_slice x22, local copies, waits for them, and re-layouts, put_group(): return holder.at[chosen].set(jnp.where(in_turn, value, holder[chosen]))  23.1 us
  transfers between devices with their start and end apart: 24, of which 21 were waited for; matrix products, arithmetic and copies ran while one was open for 10% of the time, Pallas kernels for 0%

commit v1 on v0

v1 whole, which is shorter than its diff:
```python
import functools
import math

import jax
import jax.numpy as jnp
import ml_dtypes
import numpy as np
from jax import lax
from jax.experimental import pallas as pl
from jax.experimental.pallas import tpu as pltpu
from jax.sharding import PartitionSpec as P

prop_strength = 24.0
step_rate = 0.08
MESH = pl.DeviceIdType.MESH
VMEM_LIMIT = 48 * 1024 * 1024


def operators(extent):
    counter = np.arange(extent)
    phase = (counter[:, None] * counter[None, :]) % extent
    angles = phase * (2.0 * math.pi / extent)
    fourier = (np.cos(angles) - 1j * np.sin(angles)) / math.sqrt(extent)
    freq = np.where(counter < extent // 2, counter, counter - extent) / extent
    chirp = np.exp(-1j * math.pi * prop_strength * freq * freq)
    forward = np.conj(fourier) @ (chirp[:, None] * fourier)
    forward = 0.5 * (forward + forward.T)
    packed = []
    for matrix in (forward, np.conj(forward), fourier, np.conj(fourier)):
        whole = np.block([[matrix.real, matrix.imag], [-matrix.imag, matrix.real]]).astype(np.float32)
        high = whole.astype(ml_dtypes.bfloat16)
        low = (whole - high.astype(np.float32)).astype(ml_dtypes.bfloat16)
        packed.append(np.stack([high, low]))
    return np.stack(packed)


def split(value):
    high = value.astype(jnp.bfloat16)
    return high, (value - high.astype(jnp.float32)).astype(jnp.bfloat16)


def dot(first, second):
    return jnp.dot(first, second, preferred_element_type=jnp.float32)


def transform(real, imag, op_ref, which):
    extent = real.shape[0]
    real_parts, imag_parts = split(real), split(imag)
    high, low = [
        jnp.concatenate([jnp.concatenate([r, i], 1), jnp.concatenate([-i, r], 1)], 0)
        for r, i in zip(real_parts, imag_parts)
    ]
    left_high, left_low = op_ref[which, 0, :extent], op_ref[which, 1, :extent]
    turned = dot(left_high, high) + (dot(left_high, low) + dot(left_low, high))
    high, low = split(turned)
    right_high, right_low = op_ref[which, 0], op_ref[which, 1]
    out = dot(high, right_high) + (dot(high, right_low) + dot(low, right_high))
    return out[:, :extent], out[:, extent:]


def pipeline_kernel(
    depth_count, weight_ref, window_ref, probe_ref, measured_ref, op_ref, grad_ref,
    seen, wave_grad, send_out, recv_out, send_back, recv_back,
):
    slots, _, layers = window_ref.shape[:3]
    depth_at = lax.axis_index("depth")
    last = depth_at // (depth_count - 1)
    first = depth_at == 0
    not_last = depth_at < depth_count - 1
    own_layers = layers - last

    barrier = pltpu.get_barrier_semaphore()

    @pl.when(not_last)
    def _():
        pl.semaphore_signal(barrier, inc=1, device_id={"depth": depth_at + 1}, device_id_type=MESH)

    @pl.when(depth_at > 0)
    def _():
        pl.semaphore_signal(barrier, inc=1, device_id={"depth": depth_at - 1}, device_id_type=MESH)

    pl.semaphore_wait(barrier, 2 - last - (depth_count - 1 - depth_at) // (depth_count - 1))

    def wave_copy(slot):
        return pltpu.make_async_remote_copy(
            src_ref=seen.at[slot, layers], dst_ref=seen.at[slot, 0],
            send_sem=send_out.at[slot], recv_sem=recv_out.at[slot],
            device_id={"depth": depth_at + 1}, device_id_type=MESH,
        )

    def grad_copy(slot):
        return pltpu.make_async_remote_copy(
            src_ref=wave_grad.at[slot, 0], dst_ref=wave_grad.at[slot, layers],
            send_sem=send_back.at[slot], recv_sem=recv_back.at[slot],
            device_id={"depth": depth_at - 1}, device_id_type=MESH,
        )

    def illuminated(slot, layer):
        o_real, o_imag = window_ref[slot, 0, layer], window_ref[slot, 1, layer]
        w_real, w_imag = seen[slot, layer, 0], seen[slot, layer, 1]
        return o_real * w_real - o_imag * w_imag, o_real * w_imag + o_imag * w_real

    def keep_gradients(slot, layer, g_real, g_imag):
        o_real, o_imag = window_ref[slot, 0, layer], window_ref[slot, 1, layer]
        w_real, w_imag = seen[slot, layer, 0], seen[slot, layer, 1]
        wave_grad[slot, layer, 0] = g_real * o_real + g_imag * o_imag
        wave_grad[slot, layer, 1] = g_imag * o_real - g_real * o_imag
        grad_ref[slot, 0, layer] = g_real * w_real + g_imag * w_imag
        grad_ref[slot, 1, layer] = g_imag * w_real - g_real * w_imag

    def go_out(slot):
        @pl.when(first)
        def _():
            seen[slot, 0] = probe_ref[...]

        @pl.when(depth_at > 0)
        def _():
            wave_copy(slot).wait_recv()

        @pl.loop(0, own_layers)
        def _(layer):
            real, imag = transform(*illuminated(slot, layer), op_ref, 0)
            seen[slot, layer + 1, 0] = real
            seen[slot, layer + 1, 1] = imag

        @pl.when(not_last)
        def _():
            wave_copy(slot).start()

        @pl.when(last == 1)
        def _():
            real, imag = transform(*illuminated(slot, layers - 1), op_ref, 2)
            resid = real * real + imag * imag - measured_ref[slot]
            factor = (4.0 * weight_ref[slot]) * resid
            g_real, g_imag = transform(factor * real, factor * imag, op_ref, 3)
            keep_gradients(slot, layers - 1, g_real, g_imag)

    def go_back(slot):
        @pl.when(not_last)
        def _():
            grad_copy(slot).wait_recv()

        @pl.loop(0, own_layers)
        def _(step):
            layer = own_layers - 1 - step
            g_real, g_imag = transform(
                wave_grad[slot, layer + 1, 0], wave_grad[slot, layer + 1, 1], op_ref, 1
            )
            keep_gradients(slot, layer, g_real, g_imag)

        @pl.when(depth_at > 0)
        def _():
            grad_copy(slot).start()

    @pl.loop(0, 2 * slots)
    def _(step):
        backward = last * (step % 2) + (1 - last) * (step // slots)
        slot = last * (step // 2) + (1 - last) * (step % slots)

        @pl.when(backward == 0)
        def _():
            go_out(slot)

        @pl.when(backward == 1)
        def _():
            go_back(slot)

    @pl.loop(0, slots)
    def _(slot):
        @pl.when(not_last)
        def _():
            wave_copy(slot).wait_send()

        @pl.when(depth_at > 0)
        def _():
            grad_copy(slot).wait_send()


def run_pipeline(depth_count, weights, windows, probe, measured, ops):
    slots, _, layers, extent, _ = windows.shape
    whole = pl.BlockSpec(memory_space=pltpu.VMEM)
    return pl.pallas_call(
        functools.partial(pipeline_kernel, depth_count),
        out_shape=jax.ShapeDtypeStruct(windows.shape, jnp.float32),
        in_specs=[pl.BlockSpec(memory_space=pltpu.SMEM), whole, whole, whole, whole],
        out_specs=whole,
        scratch_shapes=[
            pltpu.VMEM((slots, layers + 1, 2, extent, extent), jnp.float32),
            pltpu.VMEM((slots, layers + 1, 2, extent, extent), jnp.float32),
        ]
        + [pltpu.SemaphoreType.DMA((slots,))] * 4,
        compiler_params=pltpu.CompilerParams(
            collective_id=0, has_side_effects=True, vmem_limit_bytes=VMEM_LIMIT
        ),
        name="depth_pipeline",
    )(weights, windows, probe, measured, ops)


def cut_kernel(start_ref, above_ref, strip_ref, below_ref, out_ref):
    extent = out_ref.shape[-1]
    strip = strip_ref[0, 0]
    for slot, parts in enumerate(((above_ref[0, 0], strip), (strip, below_ref[0, 0]))):
        area = jnp.concatenate(parts, 0)
        rows, cols = area.shape
        area = pltpu.roll(area, lax.rem(rows - start_ref[slot, 0], rows), 0)[:extent]
        area = pltpu.roll(area, lax.rem(cols - start_ref[slot, 1], cols), 1)
        out_ref[slot, 0, 0] = area[:, :extent]


def cut_windows(starts, above, strip, below, extent):
    slots = starts.shape[0]
    _, layers, rows, cols = strip.shape
    half = above.shape[2]

    def spec(height):
        return pl.BlockSpec((1, 1, height, cols), lambda c, l: (c, l, 0, 0))

    return pl.pallas_call(
        cut_kernel,
        grid=(2, layers),
        out_shape=jax.ShapeDtypeStruct((slots, 2, layers, extent, extent), jnp.float32),
        in_specs=[pl.BlockSpec(memory_space=pltpu.SMEM), spec(half), spec(rows), spec(half)],
        out_specs=pl.BlockSpec((slots, 1, 1, extent, extent), lambda c, l: (0, c, l, 0, 0)),
        compiler_params=pltpu.CompilerParams(vmem_limit_bytes=VMEM_LIMIT),
        name="cut_windows",
    )(starts, above, strip, below)


def place_kernel(start_ref, grad_ref, above_ref, inner_ref, below_ref):
    half = above_ref.shape[2]
    rows, cols = inner_ref.shape[2:]
    areas = []
    for slot in range(2):
        patch = grad_ref[slot, 0, 0]
        extent = patch.shape[0]
        patch = jnp.concatenate([patch, jnp.zeros((extent, cols - extent), jnp.float32)], 1)
        patch = pltpu.roll(patch, start_ref[slot, 1], 1)
        area = jnp.concatenate([patch, jnp.zeros((rows + half - extent, cols), jnp.float32)], 0)
        areas.append(pltpu.roll(area, start_ref[slot, 0], 0))
    above_ref[0, 0] = areas[0][:half]
    inner_ref[0, 0] = areas[0][half:] + areas[1][:rows]
    below_ref[0, 0] = areas[1][rows:]


def place_gradients(starts, grads, half, rows, cols):
    slots, _, layers, extent, _ = grads.shape

    def spec(height):
        return pl.BlockSpec((1, 1, height, cols), lambda c, l: (c, l, 0, 0))

    def shape(height):
        return jax.ShapeDtypeStruct((2, layers, height, cols), jnp.float32)

    return pl.pallas_call(
        place_kernel,
        grid=(2, layers),
        out_shape=(shape(half), shape(rows), shape(half)),
        in_specs=[
            pl.BlockSpec(memory_space=pltpu.SMEM),
            pl.BlockSpec((slots, 1, 1, extent, extent), lambda c, l: (0, c, l, 0, 0)),
        ],
        out_specs=(spec(half), spec(rows), spec(half)),
        compiler_params=pltpu.CompilerParams(vmem_limit_bytes=VMEM_LIMIT),
        name="place_gradients",
    )(starts, grads)


def shards(transmission, probe, intensity, positions, batch):
    extent = probe.shape[1]
    half = extent // 2
    rows, cols = transmission.shape[2:]
    depth_count = lax.axis_size("depth")
    tiles = lax.axis_size("tile")
    tile_at = lax.axis_index("tile")
    ops = jnp.asarray(operators(extent))
    top_rows = positions[:, 0] - tile_at * rows + half
    starts = jnp.stack([top_rows - jnp.array([0, half], jnp.int32), positions[:, 1]], 1)
    down = [(i, i + 1) for i in range(tiles - 1)]
    up = [(i + 1, i) for i in range(tiles - 1)]

    strip = transmission
    for turn in range(2):
        weights = (batch == turn).astype(jnp.float32)
        above = lax.ppermute(strip[:, :, rows - half :], "tile", down)
        below = lax.ppermute(strip[:, :, :half], "tile", up)
        windows = cut_windows(starts, above, strip, below, extent)
        grads = run_pipeline(depth_count, weights, windows, probe, intensity, ops)
        to_above, inner, to_below = place_gradients(starts, grads, half, rows, cols)
        from_above = lax.ppermute(to_below, "tile", down)
        from_below = lax.ppermute(to_above, "tile", up)
        full = inner + jnp.concatenate([from_above, from_below], 2)
        strip = strip - step_rate * full
    return strip


def solution(mesh):
    return jax.shard_map(
        shards,
        mesh=mesh,
        in_specs=(
            P(None, "depth", "tile", None),
            P(),
            P("tile", None, None),
            P("tile", None),
            P("tile"),
        ),
        out_specs=P(None, "depth", "tile", None),
        check_vma=False,
    )
```

time: 862 us -> 335 us (0.39)
  the two profiles are of different devices: /device:TPU:3 before, /device:TPU:1 now
where the time goes in v1:
time: 335 us; the launch traced here: 334 us
  Pallas kernels  161 us (48%)
  starting transfers between devices  86.4 us (26%)
  waiting for transfers between devices  77.1 us (23%)
  local copies, waits for them, and re-layouts  6.85 us (2%)
    pallas_call x2, Pallas kernels, run_pipeline(): pl.pallas_call(functools.partial(pipeline_kernel, depth_count), out_shape...  142 us
    ppermute x2, starting transfers between devices, shards(): from_above = lax.ppermute(to_below, 'tile', down)  70.6 us
    ppermute x2, waiting for transfers between devices, shards(): below = lax.ppermute(strip[:, :, :half], 'tile', up)  39.7 us
    ppermute x2, waiting for transfers between devices, shards(): from_above = lax.ppermute(to_below, 'tile', down)  19.6 us
    ppermute x2, waiting for transfers between devices, shards(): from_below = lax.ppermute(to_above, 'tile', up)  17.8 us
    pallas_call x2, Pallas kernels, place_gradients(): pl.pallas_call(place_kernel, grid=(2, layers), out_shape=(shape(half), sh...  10.4 us
    pallas_call x2, Pallas kernels, cut_windows(): pl.pallas_call(cut_kernel, grid=(2, layers), out_shape=jax.ShapeDtypeStru...  8.74 us
    ppermute x2, starting transfers between devices, shards(): above = lax.ppermute(strip[:, :, rows - half:], 'tile', down)  8.11 us
  transfers between devices with their start and end apart: 8, of which 6 were waited for; matrix products, arithmetic and copies ran while one was open for 0% of the time, Pallas kernels for 0%

profile of v1, /device:TPU:1, one launch (start us, length us, event | category | flops | bytes accessed | tf_op | source)
XLA Modules:
  0.0 334.5 jit_solution(10449881008569028482)
XLA Ops:
  0.0 0.0 copy-start.7
  0.0 0.0 copy-start.8
  0.0 2.8 fusion.5
  2.8 2.0 collective-permute-start.1
  4.7 4.5 %collective-permute-start = (f32[2,2,128,512]{3,2,1,0:T(8,128)S(1)}, f32[2,2,128,512]{3,2,1,0:T(8,128)S(1)}, u32[]{:S(2)}, u32[]{:S(2)}) collective-permute-start(f32[2,2,128,512]{3,2,1,0:T(8,128)S(1)} %get-tuple-element.20), channel_id=1, source_target_pairs={{0,1},{1,2},{2,3},{3,4},{4,5},{5,6},{6,7},{8,9},{9,10},{10,11},{11... | collective-permute-start | bytes 3145736 | tf_op jit(solution)/shard_map/ppermute | solution.py:284
  9.2 0.0 copy-done.7
  9.2 0.1 add_reduce_fusion
  9.4 0.1 copy.8
  9.4 0.1 pad_add_fusion.start_ref
  9.5 0.0 copy-done.8
  9.5 0.0 copy-start.2
  9.5 0.0 copy-start.3
  9.6 18.1 %collective-permute-done.1.below_ref = f32[2,2,128,512]{3,2,1,0:T(8,128)S(1)} collective-permute-done((f32[2,2,128,512]{3,2,1,0:T(8,128)}, f32[2,2,128,512]{3,2,1,0:T(8,128)S(1)}, u32[]{:S(2)}, u32[]{:S(2)}) %collective-permute-start.1) | collective-permute-done | bytes 1048608 | tf_op jit(solution)/shard_map/ppermute | solution.py:285
  27.7 0.0 collective-permute-done.above_ref
  27.7 4.4 %cut_windows.2.window_ref = f32[2,2,2,256,256]{4,3,2,1,0:T(8,128)S(1)} custom-call(s32[2,2]{1,0:T(2,128)S(1)} %pad_add_fusion.start_ref, f32[2,2,128,512]{3,2,1,0:T(8,128)S(1)} %collective-permute-done.above_ref, f32[2,2,256,512]{3,2,1,0:T(8,128)} %strip_ref.1, f32[2,2,128,512]{3,2,1,0:T(8,128)S(1)} %collective-permute-done.1.below_ref), custom_call_target="tpu_custom_call" | custom-call | tf_op jit(solution)/shard_map/cut_windows/pallas_call | solution.py:218
  32.0 0.0 copy-done.2
  32.0 0.0 copy-done.3
  32.0 71.6 %depth_pipeline.2.grad_ref = f32[2,2,2,256,256]{4,3,2,1,0:T(8,128)S(1)} custom-call(f32[2]{0:T(128)S(1)} %get-tuple-element.24.weight_ref, f32[2,2,2,256,256]{4,3,2,1,0:T(8,128)S(1)} %cut_windows.2.window_ref, f32[2,256,256]{2,1,0:T(8,128)S(1)} %copy-done.2, f32[2,256,256]{2,1,0:T(8,128)S(1)} %copy-done.3, bf16[4,2,512,512]{3,2,1,0:T(8,128)(2,1)} %constant.19.clone.op_ref), custom_call_target="tpu_custom_call" | custom-call | tf_op jit(solution)/shard_map/depth_pipeline/pallas_call | solution.py:182
  103.7 0.0 copy-start.1
  103.7 1.3 copy-done.1
  105.0 0.0 copy-start.6
  105.0 5.2 %place_gradients.2 = (f32[2,2,128,512]{3,2,1,0:T(8,128)S(1)}, f32[2,2,256,512]{3,2,1,0:T(8,128)S(1)}, f32[2,2,128,512]{3,2,1,0:T(8,128)S(1)}) custom-call(s32[2,2]{1,0:T(2,128)S(1)} %pad_add_fusion.start_ref, f32[2,2,2,256,256]{4,3,2,1,0:T(8,128)} %copy-done.1), custom_call_target="tpu_custom_call" | custom-call | tf_op jit(solution)/shard_map/place_gradients/pallas_call | solution.py:254
  110.2 37.9 %collective-permute-start.2 = (f32[2,2,128,512]{3,2,1,0:T(8,128)S(1)}, f32[2,2,128,512]{3,2,1,0:T(8,128)S(1)}, u32[]{:S(2)}, u32[]{:S(2)}) collective-permute-start(f32[2,2,128,512]{3,2,1,0:T(8,128)S(1)} %get-tuple-element.12), channel_id=1, source_target_pairs={{0,1},{1,2},{2,3},{3,4},{4,5},{5,6},{6,7},{8,9},{9,10},{10,11},{11... | collective-permute-start | bytes 3145736 | tf_op jit(solution)/shard_map/ppermute | solution.py:289
  148.1 1.9 collective-permute-start.3
  150.1 9.8 %collective-permute-done.2 = f32[2,2,128,512]{3,2,1,0:T(8,128)S(1)} collective-permute-done((f32[2,2,128,512]{3,2,1,0:T(8,128)S(1)}, f32[2,2,128,512]{3,2,1,0:T(8,128)S(1)}, u32[]{:S(2)}, u32[]{:S(2)}) %collective-permute-start.2) | collective-permute-done | bytes 1048608 | tf_op jit(solution)/shard_map/ppermute | solution.py:289
  159.9 10.3 %collective-permute-done.3 = f32[2,2,128,512]{3,2,1,0:T(8,128)S(1)} collective-permute-done((f32[2,2,128,512]{3,2,1,0:T(8,128)S(1)}, f32[2,2,128,512]{3,2,1,0:T(8,128)S(1)}, u32[]{:S(2)}, u32[]{:S(2)}) %collective-permute-start.3) | collective-permute-done | bytes 1048608 | tf_op jit(solution)/shard_map/ppermute | solution.py:290
  170.2 0.0 copy-done.6
  170.2 0.8 fusion.1.strip_ref
  170.9 0.0 copy-start.4
  170.9 0.2 fusion.4
  171.2 1.1 copy-done.4
  172.3 1.9 collective-permute-start.5
  174.2 3.6 %collective-permute-start.4 = (f32[2,2,128,512]{3,2,1,0:T(8,128)S(1)}, f32[2,2,128,512]{3,2,1,0:T(8,128)S(1)}, u32[]{:S(2)}, u32[]{:S(2)}) collective-permute-start(f32[2,2,128,512]{3,2,1,0:T(8,128)S(1)} %get-tuple-element.18), channel_id=1, source_target_pairs={{0,1},{1,2},{2,3},{3,4},{4,5},{5,6},{6,7},{8,9},{9,10},{10,11},{11... | collective-permute-start | bytes 3145736 | tf_op jit(solution)/shard_map/ppermute | solution.py:284
  177.8 21.6 %collective-permute-done.5.below_ref = f32[2,2,128,512]{3,2,1,0:T(8,128)S(1)} collective-permute-done((f32[2,2,128,512]{3,2,1,0:T(8,128)S(1)}, f32[2,2,128,512]{3,2,1,0:T(8,128)S(1)}, u32[]{:S(2)}, u32[]{:S(2)}) %collective-permute-start.5) | collective-permute-done | bytes 1048608 | tf_op jit(solution)/shard_map/ppermute | solution.py:285
  199.4 0.0 collective-permute-done.4.above_ref
  199.4 4.4 %cut_windows.3.window_ref = f32[2,2,2,256,256]{4,3,2,1,0:T(8,128)S(1)} custom-call(s32[2,2]{1,0:T(2,128)S(1)} %pad_add_fusion.start_ref, f32[2,2,128,512]{3,2,1,0:T(8,128)S(1)} %collective-permute-done.4.above_ref, f32[2,2,256,512]{3,2,1,0:T(8,128)} %copy-done.4, f32[2,2,128,512]{3,2,1,0:T(8,128)S(1)} %collective-permute-done.5.below_ref), custom_call_target="tpu_custom_call" | custom-call | tf_op jit(solution)/shard_map/cut_windows/pallas_call | solution.py:218
  203.8 70.1 %depth_pipeline.3.grad_ref = f32[2,2,2,256,256]{4,3,2,1,0:T(8,128)S(1)} custom-call(f32[2]{0:T(128)S(1)} %get-tuple-element.23.weight_ref, f32[2,2,2,256,256]{4,3,2,1,0:T(8,128)S(1)} %cut_windows.3.window_ref, f32[2,256,256]{2,1,0:T(8,128)S(1)} %copy-done.2, f32[2,256,256]{2,1,0:T(8,128)S(1)} %copy-done.3, bf16[4,2,512,512]{3,2,1,0:T(8,128)(2,1)} %constant.19.clone.op_ref), custom_call_target="tpu_custom_call" | custom-call | tf_op jit(solution)/shard_map/depth_pipeline/pallas_call | solution.py:182
  273.9 0.0 copy-start
  273.9 1.3 copy-done
  275.3 0.0 copy-start.5
  275.3 5.2 %place_gradients.3 = (f32[2,2,128,512]{3,2,1,0:T(8,128)S(1)}, f32[2,2,256,512]{3,2,1,0:T(8,128)S(1)}, f32[2,2,128,512]{3,2,1,0:T(8,128)S(1)}) custom-call(s32[2,2]{1,0:T(2,128)S(1)} %pad_add_fusion.start_ref, f32[2,2,2,256,256]{4,3,2,1,0:T(8,128)} %copy-done), custom_call_target="tpu_custom_call" | custom-call | tf_op jit(solution)/shard_map/place_gradients/pallas_call | solution.py:254
  280.5 32.6 %collective-permute-start.6 = (f32[2,2,128,512]{3,2,1,0:T(8,128)S(1)}, f32[2,2,128,512]{3,2,1,0:T(8,128)S(1)}, u32[]{:S(2)}, u32[]{:S(2)}) collective-permute-start(f32[2,2,128,512]{3,2,1,0:T(8,128)S(1)} %get-tuple-element.15), channel_id=1, source_target_pairs={{0,1},{1,2},{2,3},{3,4},{4,5},{5,6},{6,7},{8,9},{9,10},{10,11},{11... | collective-permute-start | bytes 3145736 | tf_op jit(solution)/shard_map/ppermute | solution.py:289
  313.1 1.9 collective-permute-start.7
  315.1 9.8 %collective-permute-done.6 = f32[2,2,128,512]{3,2,1,0:T(8,128)S(1)} collective-permute-done((f32[2,2,128,512]{3,2,1,0:T(8,128)S(1)}, f32[2,2,128,512]{3,2,1,0:T(8,128)S(1)}, u32[]{:S(2)}, u32[]{:S(2)}) %collective-permute-start.6) | collective-permute-done | bytes 1048608 | tf_op jit(solution)/shard_map/ppermute | solution.py:289
  324.9 7.5 %collective-permute-done.7 = f32[2,2,128,512]{3,2,1,0:T(8,128)S(1)} collective-permute-done((f32[2,2,128,512]{3,2,1,0:T(8,128)S(1)}, f32[2,2,128,512]{3,2,1,0:T(8,128)S(1)}, u32[]{:S(2)}, u32[]{:S(2)}) %collective-permute-start.7) | collective-permute-done | bytes 1048608 | tf_op jit(solution)/shard_map/ppermute | solution.py:290
  332.4 0.0 copy-done.5
  332.4 2.1 fusion.3
  (2 shorter events, 0.0 us)
Async XLA Ops:
  0.0 9.2 %copy-start.7 = (s32[2,2]{1,0:T(2,128)S(1)}, s32[2,2]{1,0:T(2,128)}, u32[]{:S(2)}) copy-start(s32[2,2]{1,0:T(2,128)} %param.10) | copy-start | bytes 52
  0.0 9.5 %copy-start.8 = (s32[2]{0:T(128)S(1)}, s32[2]{0:T(128)}, u32[]{:S(2)}) copy-start(s32[2]{0:T(128)} %param.11) | copy-start | bytes 28
  2.8 24.9 %collective-permute-start.1 = (f32[2,2,128,512]{3,2,1,0:T(8,128)}, f32[2,2,128,512]{3,2,1,0:T(8,128)S(1)}, u32[]{:S(2)}, u32[]{:S(2)}) collective-permute-start(f32[2,2,128,512]{3,2,1,0:T(8,128)} %get-tuple-element.19), channel_id=1, source_target_pairs={{1,0},{2,1},{3,2},{4,3},{5,4},{6,5},{7,6},{9,8},{10,9},{11,10},{12... | collective-permute-start | bytes 3145736 | tf_op jit(solution)/shard_map/ppermute | solution.py:285
  4.7 22.9 %collective-permute-start = (f32[2,2,128,512]{3,2,1,0:T(8,128)S(1)}, f32[2,2,128,512]{3,2,1,0:T(8,128)S(1)}, u32[]{:S(2)}, u32[]{:S(2)}) collective-permute-start(f32[2,2,128,512]{3,2,1,0:T(8,128)S(1)} %get-tuple-element.20), channel_id=1, source_target_pairs={{0,1},{1,2},{2,3},{3,4},{4,5},{5,6},{6,7},{8,9},{9,10},{10,11},{11... | collective-permute-start | bytes 3145736 | tf_op jit(solution)/shard_map/ppermute | solution.py:284
  9.5 22.5 %copy-start.2 = (f32[2,256,256]{2,1,0:T(8,128)S(1)}, f32[2,256,256]{2,1,0:T(8,128)}, u32[]{:S(2)}) copy-start(f32[2,256,256]{2,1,0:T(8,128)} %probe_ref.3) | copy-start | bytes 1572868
  9.5 22.5 %copy-start.3 = (f32[2,256,256]{2,1,0:T(8,128)S(1)}, f32[2,256,256]{2,1,0:T(8,128)}, u32[]{:S(2)}) copy-start(f32[2,256,256]{2,1,0:T(8,128)} %measured_ref.3) | copy-start | bytes 1572868
  103.7 1.3 copy-start.1
  105.0 65.2 %copy-start.6 = (f32[2,2,256,512]{3,2,1,0:T(8,128)S(1)}, f32[2,2,256,512]{3,2,1,0:T(8,128)}, u32[]{:S(2)}) copy-start(f32[2,2,256,512]{3,2,1,0:T(8,128)} %strip_ref.1) | copy-start | bytes 6291460
  110.2 49.6 %collective-permute-start.2 = (f32[2,2,128,512]{3,2,1,0:T(8,128)S(1)}, f32[2,2,128,512]{3,2,1,0:T(8,128)S(1)}, u32[]{:S(2)}, u32[]{:S(2)}) collective-permute-start(f32[2,2,128,512]{3,2,1,0:T(8,128)S(1)} %get-tuple-element.12), channel_id=1, source_target_pairs={{0,1},{1,2},{2,3},{3,4},{4,5},{5,6},{6,7},{8,9},{9,10},{10,11},{11... | collective-permute-start | bytes 3145736 | tf_op jit(solution)/shard_map/ppermute | solution.py:289
  148.1 22.0 %collective-permute-start.3 = (f32[2,2,128,512]{3,2,1,0:T(8,128)S(1)}, f32[2,2,128,512]{3,2,1,0:T(8,128)S(1)}, u32[]{:S(2)}, u32[]{:S(2)}) collective-permute-start(f32[2,2,128,512]{3,2,1,0:T(8,128)S(1)} %get-tuple-element.13), channel_id=1, source_target_pairs={{1,0},{2,1},{3,2},{4,3},{5,4},{6,5},{7,6},{9,8},{10,9},{11,10},{12... | collective-permute-start | bytes 3145736 | tf_op jit(solution)/shard_map/ppermute | solution.py:290
  170.9 1.3 copy-start.4
  172.3 27.2 %collective-permute-start.5 = (f32[2,2,128,512]{3,2,1,0:T(8,128)S(1)}, f32[2,2,128,512]{3,2,1,0:T(8,128)S(1)}, u32[]{:S(2)}, u32[]{:S(2)}) collective-permute-start(f32[2,2,128,512]{3,2,1,0:T(8,128)S(1)} %get-tuple-element.17), channel_id=1, source_target_pairs={{1,0},{2,1},{3,2},{4,3},{5,4},{6,5},{7,6},{9,8},{10,9},{11,10},{12... | collective-permute-start | bytes 3145736 | tf_op jit(solution)/shard_map/ppermute | solution.py:285
  174.2 25.3 %collective-permute-start.4 = (f32[2,2,128,512]{3,2,1,0:T(8,128)S(1)}, f32[2,2,128,512]{3,2,1,0:T(8,128)S(1)}, u32[]{:S(2)}, u32[]{:S(2)}) collective-permute-start(f32[2,2,128,512]{3,2,1,0:T(8,128)S(1)} %get-tuple-element.18), channel_id=1, source_target_pairs={{0,1},{1,2},{2,3},{3,4},{4,5},{5,6},{6,7},{8,9},{9,10},{10,11},{11... | collective-permute-start | bytes 3145736 | tf_op jit(solution)/shard_map/ppermute | solution.py:284
  273.9 1.3 copy-start
  275.3 57.1 %copy-start.5 = (f32[2,2,256,512]{3,2,1,0:T(8,128)S(1)}, f32[2,2,256,512]{3,2,1,0:T(8,128)}, u32[]{:S(2)}) copy-start(f32[2,2,256,512]{3,2,1,0:T(8,128)} %copy-done.4) | copy-start | bytes 6291460
  280.5 44.4 %collective-permute-start.6 = (f32[2,2,128,512]{3,2,1,0:T(8,128)S(1)}, f32[2,2,128,512]{3,2,1,0:T(8,128)S(1)}, u32[]{:S(2)}, u32[]{:S(2)}) collective-permute-start(f32[2,2,128,512]{3,2,1,0:T(8,128)S(1)} %get-tuple-element.15), channel_id=1, source_target_pairs={{0,1},{1,2},{2,3},{3,4},{4,5},{5,6},{6,7},{8,9},{9,10},{10,11},{11... | collective-permute-start | bytes 3145736 | tf_op jit(solution)/shard_map/ppermute | solution.py:289
  313.1 19.3 %collective-permute-start.7 = (f32[2,2,128,512]{3,2,1,0:T(8,128)S(1)}, f32[2,2,128,512]{3,2,1,0:T(8,128)S(1)}, u32[]{:S(2)}, u32[]{:S(2)}) collective-permute-start(f32[2,2,128,512]{3,2,1,0:T(8,128)S(1)} %get-tuple-element.16), channel_id=1, source_target_pairs={{1,0},{2,1},{3,2},{4,3},{5,4},{6,5},{7,6},{9,8},{10,9},{11,10},{12... | collective-permute-start | bytes 3145736 | tf_op jit(solution)/shard_map/ppermute | solution.py:290

commit v2 on v1

v2 whole, which is shorter than its diff:
```python
import functools
import math

import jax
import jax.numpy as jnp
import ml_dtypes
import numpy as np
from jax import lax
from jax.experimental import pallas as pl
from jax.experimental.pallas import tpu as pltpu
from jax.sharding import PartitionSpec as P

prop_strength = 24.0
step_rate = 0.08
MESH = pl.DeviceIdType.MESH
VMEM_LIMIT = 48 * 1024 * 1024


def operators(extent):
    counter = np.arange(extent)
    phase = (counter[:, None] * counter[None, :]) % extent
    angles = phase * (2.0 * math.pi / extent)
    fourier = (np.cos(angles) - 1j * np.sin(angles)) / math.sqrt(extent)
    freq = np.where(counter < extent // 2, counter, counter - extent) / extent
    chirp = np.exp(-1j * math.pi * prop_strength * freq * freq)
    forward = np.conj(fourier) @ (chirp[:, None] * fourier)
    forward = 0.5 * (forward + forward.T)
    packed = []
    for matrix in (forward, np.conj(forward), fourier, np.conj(fourier)):
        whole = np.block([[matrix.real, matrix.imag], [-matrix.imag, matrix.real]]).astype(np.float32)
        high = whole.astype(ml_dtypes.bfloat16)
        low = (whole - high.astype(np.float32)).astype(ml_dtypes.bfloat16)
        packed.append(np.stack([high, low]))
    return np.stack(packed)


def split(value):
    high = value.astype(jnp.bfloat16)
    return high, (value - high.astype(jnp.float32)).astype(jnp.bfloat16)


def dot(first, second):
    return jnp.dot(first, second, preferred_element_type=jnp.float32)


def transform(real, imag, op_ref, which):
    extent = real.shape[0]
    real_parts, imag_parts = split(real), split(imag)
    high, low = [
        jnp.concatenate([jnp.concatenate([r, i], 1), jnp.concatenate([-i, r], 1)], 0)
        for r, i in zip(real_parts, imag_parts)
    ]
    left_high, left_low = op_ref[which, 0, :extent], op_ref[which, 1, :extent]
    turned = dot(left_high, high) + (dot(left_high, low) + dot(left_low, high))
    high, low = split(turned)
    right_high, right_low = op_ref[which, 0], op_ref[which, 1]
    out = dot(high, right_high) + (dot(high, right_low) + dot(low, right_high))
    return out[:, :extent], out[:, extent:]


def whole_kernel(
    depth_count, tiles, start_ref, near_ref, weight_ref, object_ref, probe_ref, measured_ref, op_ref, strip_ref,
    window, patch_grad, seen, wave_grad, halo_out, halo_in, rim_out, rim_in,
    wave_send, wave_recv, back_send, back_recv, halo_send, halo_recv, rim_send, rim_recv,
):
    phases, slots, _, _, extent, _ = seen.shape
    layers, rows, cols = object_ref.shape[1:]
    half = extent // 2
    area_rows = half + rows
    depth_at = lax.axis_index("depth")
    tile_at = lax.axis_index("tile")
    last = depth_at // (depth_count - 1)
    not_last = depth_at < depth_count - 1
    has_above = tile_at > 0
    has_below = tile_at < tiles - 1
    own_layers = layers - last
    links = (
        (not_last, {"depth": depth_at + 1}),
        (depth_at > 0, {"depth": depth_at - 1}),
        (has_below, {"tile": tile_at + 1}),
        (has_above, {"tile": tile_at - 1}),
    )
    ends = last + (depth_count - 1 - depth_at) // (depth_count - 1)
    ends = ends + tile_at // (tiles - 1) + (tiles - 1 - tile_at) // (tiles - 1)

    barrier = pltpu.get_barrier_semaphore()
    for there, device in links:

        @pl.when(there)
        def _():
            pl.semaphore_signal(barrier, inc=1, device_id=device, device_id_type=MESH)

    strip_ref[...] = object_ref[...]
    reaches = (has_above, has_below)
    serves = (has_below, has_above)
    for slot in range(2):

        @pl.when(jnp.logical_not(reaches[slot]))
        def _():
            for phase in range(phases):
                halo_in[phase, slot] = jnp.zeros(halo_in.shape[2:], jnp.float32)

        @pl.when(jnp.logical_not(serves[slot]))
        def _():
            for phase in range(phases):
                rim_in[phase, slot] = jnp.zeros(rim_in.shape[2:], jnp.float32)

    pl.semaphore_wait(barrier, 4 - ends)

    def wave_copy(phase, slot):
        return pltpu.make_async_remote_copy(
            src_ref=seen.at[phase, slot, layers], dst_ref=seen.at[phase, slot, 0],
            send_sem=wave_send.at[phase, slot], recv_sem=wave_recv.at[phase, slot],
            device_id=links[0][1], device_id_type=MESH,
        )

    def back_copy(phase, slot):
        return pltpu.make_async_remote_copy(
            src_ref=wave_grad.at[phase, slot, 0], dst_ref=wave_grad.at[phase, slot, layers],
            send_sem=back_send.at[phase, slot], recv_sem=back_recv.at[phase, slot],
            device_id=links[1][1], device_id_type=MESH,
        )

    def halo_copy(phase, side, layer):
        return pltpu.make_async_remote_copy(
            src_ref=halo_out.at[phase, side, layer], dst_ref=halo_in.at[phase, side, layer],
            send_sem=halo_send.at[phase, side, layer], recv_sem=halo_recv.at[phase, side, layer],
            device_id=links[2 + side][1], device_id_type=MESH,
        )

    def rim_copy(phase, slot, layer):
        return pltpu.make_async_remote_copy(
            src_ref=rim_out.at[phase, slot, layer], dst_ref=rim_in.at[phase, slot, layer],
            send_sem=rim_send.at[phase, slot, layer], recv_sem=rim_recv.at[phase, slot, layer],
            device_id=links[3 - slot][1], device_id_type=MESH,
        )

    def send_halo(phase, side, layer):
        base = rows - half if side == 0 else 0
        for part in range(2):
            piece = strip_ref[part, layer, base : base + half]
            piece = pltpu.roll(piece, lax.rem(cols - near_ref[side], cols), 1)
            halo_out[phase, side, layer, part] = piece[:, :extent]

        @pl.when(serves[side])
        def _():
            halo_copy(phase, side, layer).start()

    def cut_window(phase, slot, layer):
        shift = lax.rem(2 * area_rows - start_ref[slot, 0], area_rows)
        for part in range(2):
            own = pltpu.roll(strip_ref[part, layer], lax.rem(cols - start_ref[slot, 1], cols), 1)
            area = jnp.concatenate([halo_in[phase, slot, layer, part], own[:, :extent]], 0)
            window[slot, part, layer] = pltpu.roll(area, shift, 0)[:extent]

    def apply_gradients(phase, slot):
        @pl.loop(0, layers)
        def _(layer):
            for part in range(2):
                patch = patch_grad[slot, part, layer] * step_rate
                area = jnp.concatenate([patch, jnp.zeros((area_rows - extent, extent), jnp.float32)], 0)
                area = pltpu.roll(area, lax.rem(start_ref[slot, 0], area_rows), 0)
                rim_out[phase, slot, layer, part] = area[:half]
                own = jnp.concatenate([area[half:], jnp.zeros((rows, cols - extent), jnp.float32)], 1)
                strip_ref[part, layer] -= pltpu.roll(own, start_ref[slot, 1], 1)

            @pl.when(reaches[slot])
            def _():
                rim_copy(phase, slot, layer).start()

    def take_rim(phase, side, layer):
        @pl.when(serves[side])
        def _():
            rim_copy(phase, side, layer).wait_recv()

        base = rows - half if side == 0 else 0
        for part in range(2):
            piece = rim_in[phase, side, layer, part]
            piece = jnp.concatenate([piece, jnp.zeros((half, cols - extent), jnp.float32)], 1)
            strip_ref[part, layer, base : base + half] -= pltpu.roll(piece, near_ref[side], 1)

    def illuminated(phase, slot, layer):
        o_real, o_imag = window[slot, 0, layer], window[slot, 1, layer]
        w_real, w_imag = seen[phase, slot, layer, 0], seen[phase, slot, layer, 1]
        return o_real * w_real - o_imag * w_imag, o_real * w_imag + o_imag * w_real

    def keep_gradients(phase, slot, layer, g_real, g_imag):
        o_real, o_imag = window[slot, 0, layer], window[slot, 1, layer]
        w_real, w_imag = seen[phase, slot, layer, 0], seen[phase, slot, layer, 1]
        wave_grad[phase, slot, layer, 0] = g_real * o_real + g_imag * o_imag
        wave_grad[phase, slot, layer, 1] = g_imag * o_real - g_real * o_imag
        patch_grad[slot, 0, layer] = g_real * w_real + g_imag * w_imag
        patch_grad[slot, 1, layer] = g_imag * w_real - g_real * w_imag

    def go_out(phase, slot):
        @pl.when(depth_at == 0)
        def _():
            seen[phase, slot, 0] = probe_ref[...]

        @pl.when(depth_at > 0)
        def _():
            wave_copy(phase, slot).wait_recv()

        @pl.loop(0, own_layers)
        def _(layer):
            real, imag = transform(*illuminated(phase, slot, layer), op_ref, 0)
            seen[phase, slot, layer + 1, 0] = real
            seen[phase, slot, layer + 1, 1] = imag

        @pl.when(not_last)
        def _():
            wave_copy(phase, slot).start()

        @pl.when(last == 1)
        def _():
            real, imag = transform(*illuminated(phase, slot, layers - 1), op_ref, 2)
            resid = real * real + imag * imag - measured_ref[slot]
            factor = (4.0 * weight_ref[phase, slot]) * resid
            g_real, g_imag = transform(factor * real, factor * imag, op_ref, 3)
            keep_gradients(phase, slot, layers - 1, g_real, g_imag)

    def go_back(phase, slot):
        @pl.when(not_last)
        def _():
            back_copy(phase, slot).wait_recv()

        @pl.loop(0, own_layers)
        def _(step):
            layer = own_layers - 1 - step
            g_real, g_imag = transform(
                wave_grad[phase, slot, layer + 1, 0], wave_grad[phase, slot, layer + 1, 1], op_ref, 1
            )
            keep_gradients(phase, slot, layer, g_real, g_imag)

        @pl.when(depth_at > 0)
        def _():
            back_copy(phase, slot).start()

    @pl.loop(0, layers)
    def _(layer):
        for side in range(2):
            send_halo(0, side, layer)

    @pl.loop(0, phases)
    def _(phase):
        @pl.loop(0, layers)
        def _(layer):
            for slot in range(2):

                @pl.when(reaches[slot])
                def _():
                    halo_copy(phase, slot, layer).wait_recv()

                cut_window(phase, slot, layer)

        @pl.loop(0, 2 * slots)
        def _(step):
            backward = last * (step % 2) + (1 - last) * (step // slots)
            slot_at = last * (step // 2) + (1 - last) * (step % slots)

            @pl.when(backward == 0)
            def _():
                go_out(phase, slot_at)

            @pl.when(backward == 1)
            def _():
                go_back(phase, slot_at)
                for slot in range(2):

                    @pl.when(slot_at == slot)
                    def _():
                        apply_gradients(phase, slot)

        @pl.loop(0, layers)
        def _(layer):
            for side in range(2):
                take_rim(phase, side, layer)

                @pl.when(phase < phases - 1)
                def _():
                    send_halo(phase + 1, side, layer)

    @pl.loop(0, phases)
    def _(phase):
        for slot in range(2):

            @pl.when(not_last)
            def _():
                wave_copy(phase, slot).wait_send()

            @pl.when(depth_at > 0)
            def _():
                back_copy(phase, slot).wait_send()

            @pl.loop(0, layers)
            def _(layer):
                @pl.when(serves[slot])
                def _():
                    halo_copy(phase, slot, layer).wait_send()

                @pl.when(reaches[slot])
                def _():
                    rim_copy(phase, slot, layer).wait_send()


def shards(transmission, probe, intensity, positions, batch):
    extent = probe.shape[1]
    half = extent // 2
    slots = intensity.shape[0]
    _, layers, rows, _ = transmission.shape
    depth_count = lax.axis_size("depth")
    tiles = lax.axis_size("tile")
    tile_at = lax.axis_index("tile")
    phases = 2
    ops = jnp.asarray(operators(extent))
    top_rows = positions[:, 0] - tile_at * rows + half
    starts = jnp.stack([top_rows, positions[:, 1]], 1)
    near = jnp.concatenate([
        lax.ppermute(positions[:1, 1], "tile", [(i + 1, i) for i in range(tiles - 1)]),
        lax.ppermute(positions[1:, 1], "tile", [(i, i + 1) for i in range(tiles - 1)]),
    ])
    weights = (batch[None] == jnp.arange(phases, dtype=batch.dtype)[:, None]).astype(jnp.float32)
    whole = pl.BlockSpec(memory_space=pltpu.VMEM)
    scalars = pl.BlockSpec(memory_space=pltpu.SMEM)
    edge = pltpu.VMEM((phases, 2, layers, 2, half, extent), jnp.float32)
    waves = pltpu.VMEM((phases, slots, layers + 1, 2, extent, extent), jnp.float32)
    patches = pltpu.VMEM((slots, 2, layers, extent, extent), jnp.float32)
    return pl.pallas_call(
        functools.partial(whole_kernel, depth_count, tiles),
        out_shape=jax.ShapeDtypeStruct(transmission.shape, jnp.float32),
        in_specs=[scalars, scalars, scalars, whole, whole, whole, whole],
        out_specs=whole,
        scratch_shapes=[patches, patches, waves, waves, edge, edge, edge, edge]
        + [pltpu.SemaphoreType.DMA((phases, slots))] * 4
        + [pltpu.SemaphoreType.DMA((phases, slots, layers))] * 4,
        compiler_params=pltpu.CompilerParams(
            collective_id=0, has_side_effects=True, vmem_limit_bytes=VMEM_LIMIT
        ),
        name="two_minibatches",
    )(starts, near, weights, transmission, probe, intensity, ops)


def solution(mesh):
    return jax.shard_map(
        shards,
        mesh=mesh,
        in_specs=(
            P(None, "depth", "tile", None),
            P(),
            P("tile", None, None),
            P("tile", None),
            P("tile"),
        ),
        out_specs=P(None, "depth", "tile", None),
        check_vma=False,
    )
```

time: 335 us -> 230 us (0.69)
  the two profiles are of different devices: /device:TPU:1 before, /device:TPU:3 now
where the time goes in v2:
time: 230 us
  Pallas kernels  214 us (93%)
  starting transfers between devices  6.45 us (3%)
  local copies, waits for them, and re-layouts  6.41 us (3%)
  other arithmetic  2.88 us (1%)
    pallas_call x1, Pallas kernels, shards(): pl.pallas_call(functools.partial(whole_kernel, depth_count, tiles), out_s...  214 us
    unnamed x7, local copies, waits for them, and re-layouts  4.99 us
  transfers between devices with their start and end apart: 2, of which 0 were waited for; matrix products, arithmetic and copies ran while one was open for 1% of the time, Pallas kernels for 0%

profile of v2, /device:TPU:3, one launch (start us, length us, event | category | flops | bytes accessed | tf_op | source)
XLA Modules:
  0.0 229.7 jit_solution(712969721216398672)
XLA Ops:
  0.0 1.4 fusion
  1.4 2.6 %collective-permute-start = (s32[1]{0:T(128)}, s32[1]{0:T(128)}, u32[]{:S(2)}, u32[]{:S(2)}) collective-permute-start(s32[1]{0:T(128)} %bitcast), channel_id=1, source_target_pairs={{1,0},{2,1},{3,2},{4,3},{5,4},{6,5},{7,6},{9,8},{10,9},{11,10},{12... | collective-permute-start | bytes 20 | tf_op jit(solution)/shard_map/ppermute | solution.py:319
  4.0 3.9 %collective-permute-start.1 = (s32[1]{0:T(128)}, s32[1]{0:T(128)}, u32[]{:S(2)}, u32[]{:S(2)}) collective-permute-start(s32[1]{0:T(128)} %bitcast.1), channel_id=1, source_target_pairs={{0,1},{1,2},{2,3},{3,4},{4,5},{5,6},{6,7},{8,9},{9,10},{10,11},{11... | collective-permute-start | bytes 20 | tf_op jit(solution)/shard_map/ppermute | solution.py:320
  7.9 0.7 compare_convert_fusion.weight_ref
  8.6 0.8 subtract_add_fusion
  9.4 0.1 pad_add_fusion.start_ref
  9.5 0.0 collective-permute-done
  9.5 0.0 collective-permute-done.1
  9.5 1.3 pad_add_fusion.1.near_ref
  10.8 0.0 copy-start
  10.8 1.6 copy-done
  12.4 0.0 copy-start.1
  12.4 1.0 copy-done.1
  13.4 0.0 copy-start.2
  13.4 1.0 copy-done.2
  14.5 214.0 %two_minibatches.1 = f32[2,2,256,512]{3,2,1,0:T(8,128)S(1)} custom-call(s32[2,2]{1,0:T(2,128)S(1)} %pad_add_fusion.start_ref, s32[2]{0:T(128)S(1)} %pad_add_fusion.1.near_ref, f32[2,2]{1,0:T(2,128)S(1)} %compare_convert_fusion.weight_ref, f32[2,2,256,512]{3,2,1,0:T(8,128)S(1)} %copy-done, f32[2,256,256]{2,1,0:T(8,128)S(1)} %copy-done.1, ...), custom_call_target="tpu_custom_call" | custom-call | tf_op jit(solution)/shard_map/two_minibatches/pallas_call | solution.py:328
  228.4 1.3 copy.8
Async XLA Ops:
  1.4 8.0 %collective-permute-start = (s32[1]{0:T(128)}, s32[1]{0:T(128)}, u32[]{:S(2)}, u32[]{:S(2)}) collective-permute-start(s32[1]{0:T(128)} %bitcast), channel_id=1, source_target_pairs={{1,0},{2,1},{3,2},{4,3},{5,4},{6,5},{7,6},{9,8},{10,9},{11,10},{12... | collective-permute-start | bytes 20 | tf_op jit(solution)/shard_map/ppermute | solution.py:319
  4.0 5.5 %collective-permute-start.1 = (s32[1]{0:T(128)}, s32[1]{0:T(128)}, u32[]{:S(2)}, u32[]{:S(2)}) collective-permute-start(s32[1]{0:T(128)} %bitcast.1), channel_id=1, source_target_pairs={{0,1},{1,2},{2,3},{3,4},{4,5},{5,6},{6,7},{8,9},{9,10},{10,11},{11... | collective-permute-start | bytes 20 | tf_op jit(solution)/shard_map/ppermute | solution.py:320
  10.8 1.6 copy-start
  12.4 1.0 copy-start.1
  13.4 1.0 copy-start.2

commit v3 on v2

--- a/solution.py
+++ b/solution.py
@@ -61,7 +61,7 @@
 def whole_kernel(
     depth_count, tiles, start_ref, near_ref, weight_ref, object_ref, probe_ref, measured_ref, op_ref, strip_ref,
     window, patch_grad, seen, wave_grad, halo_out, halo_in, rim_out, rim_in,
-    wave_send, wave_recv, back_send, back_recv, halo_send, halo_recv, rim_send, rim_recv,
+    wave_send, wave_recv, back_send, back_recv, halo_send, halo_recv, rim_send, rim_recv, turn,
 ):
     phases, slots, _, _, extent, _ = seen.shape
     layers, rows, cols = object_ref.shape[1:]
@@ -74,13 +74,16 @@
     has_above = tile_at > 0
     has_below = tile_at < tiles - 1
     own_layers = layers - last
+    parity = tile_at % 2
+    partner = tile_at + 1 - 2 * parity
     links = (
         (not_last, {"depth": depth_at + 1}),
         (depth_at > 0, {"depth": depth_at - 1}),
         (has_below, {"tile": tile_at + 1}),
         (has_above, {"tile": tile_at - 1}),
     )
-    ends = last + (depth_count - 1 - depth_at) // (depth_count - 1)
+    start_depth = (depth_count - 1 - depth_at) // (depth_count - 1)
+    ends = last + start_depth
     ends = ends + tile_at // (tiles - 1) + (tiles - 1 - tile_at) // (tiles - 1)
 
     barrier = pltpu.get_barrier_semaphore()
@@ -192,6 +195,28 @@
         patch_grad[slot, 0, layer] = g_real * w_real + g_imag * w_imag
         patch_grad[slot, 1, layer] = g_imag * w_real - g_real * w_imag
 
+    def pass_turn(phase, slot):
+        wave_copy(phase, slot).wait_send()
+
+        @pl.when((parity == 0) | (slot < slots - 1))
+        def _():
+            pl.semaphore_signal(turn, inc=1, device_id={"tile": partner}, device_id_type=MESH)
+
+    def send_in_turn(phase, slot):
+        @pl.when(slot > 0)
+        def _():
+            pass_turn(phase, slot - 1)
+
+        @pl.when((parity == 1) | (slot > 0))
+        def _():
+            pl.semaphore_wait(turn, 1)
+
+        wave_copy(phase, slot).start()
+
+        @pl.when(slot == slots - 1)
+        def _():
+            pass_turn(phase, slot)
+
     def go_out(phase, slot):
         @pl.when(depth_at == 0)
         def _():
@@ -207,7 +232,11 @@
             seen[phase, slot, layer + 1, 0] = real
             seen[phase, slot, layer + 1, 1] = imag
 
-        @pl.when(not_last)
+        @pl.when(depth_at == 0)
+        def _():
+            send_in_turn(phase, slot)
+
+        @pl.when(not_last & (depth_at > 0))
         def _():
             wave_copy(phase, slot).start()
 
@@ -243,21 +272,25 @@
 
     @pl.loop(0, phases)
     def _(phase):
-        @pl.loop(0, layers)
-        def _(layer):
-            for slot in range(2):
-
-                @pl.when(reaches[slot])
-                def _():
-                    halo_copy(phase, slot, layer).wait_recv()
-
-                cut_window(phase, slot, layer)
-
         @pl.loop(0, 2 * slots)
         def _(step):
             backward = last * (step % 2) + (1 - last) * (step // slots)
             slot_at = last * (step // 2) + (1 - last) * (step % slots)
 
+            @pl.when((step < slots) & ((start_depth == 1) | (step == 0)))
+            def _():
+                @pl.loop(step, step + 1 + (1 - start_depth) * (slots - 1))
+                def _(cut_slot):
+                    @pl.loop(0, layers)
+                    def _(layer):
+                        for slot in range(2):
+
+                            @pl.when((cut_slot == slot) & reaches[slot])
+                            def _():
+                                halo_copy(phase, slot, layer).wait_recv()
+
+                        cut_window(phase, cut_slot, layer)
+
             @pl.when(backward == 0)
             def _():
                 go_out(phase, slot_at)
@@ -271,9 +304,10 @@
                     def _():
                         apply_gradients(phase, slot)
 
-        @pl.loop(0, layers)
-        def _(layer):
-            for side in range(2):
+        for side in range(2):
+
+            @pl.loop(0, layers)
+            def _(layer):
                 take_rim(phase, side, layer)
 
                 @pl.when(phase < phases - 1)
@@ -284,7 +318,7 @@
     def _(phase):
         for slot in range(2):
 
-            @pl.when(not_last)
+            @pl.when(not_last & (depth_at > 0))
             def _():
                 wave_copy(phase, slot).wait_send()
 
@@ -332,7 +366,8 @@
         out_specs=whole,
         scratch_shapes=[patches, patches, waves, waves, edge, edge, edge, edge]
         + [pltpu.SemaphoreType.DMA((phases, slots))] * 4
-        + [pltpu.SemaphoreType.DMA((phases, slots, layers))] * 4,
+        + [pltpu.SemaphoreType.DMA((phases, slots, layers))] * 4
+        + [pltpu.SemaphoreType.REGULAR],
         compiler_params=pltpu.CompilerParams(
             collective_id=0, has_side_effects=True, vmem_limit_bytes=VMEM_LIMIT
         ),

time: 230 us -> 234 us (1.017)
  the two profiles are of different devices: /device:TPU:3 before, /device:TPU:7 now
where the time goes in v3:
time: 234 us
  Pallas kernels  220 us (94%)
  local copies, waits for them, and re-layouts  6.41 us (3%)
  starting transfers between devices  4.43 us (2%)
  other arithmetic  2.87 us (1%)
    pallas_call x1, Pallas kernels, shards(): pl.pallas_call(functools.partial(whole_kernel, depth_count, tiles), out_s...  220 us
    unnamed x7, local copies, waits for them, and re-layouts  4.99 us
  transfers between devices with their start and end apart: 2, of which 1 were waited for; matrix products, arithmetic and copies ran while one was open for 1% of the time, Pallas kernels for 0%

profile of v3, /device:TPU:7, one launch (start us, length us, event | category | flops | bytes accessed | tf_op | source)
XLA Modules:
  0.0 234.0 jit_solution(13020421701823227234)
XLA Ops:
  0.0 1.4 fusion
  1.4 3.1 %collective-permute-start = (s32[1]{0:T(128)}, s32[1]{0:T(128)}, u32[]{:S(2)}, u32[]{:S(2)}) collective-permute-start(s32[1]{0:T(128)} %bitcast), channel_id=1, source_target_pairs={{1,0},{2,1},{3,2},{4,3},{5,4},{6,5},{7,6},{9,8},{10,9},{11,10},{12... | collective-permute-start | bytes 20 | tf_op jit(solution)/shard_map/ppermute | solution.py:353
  4.6 1.3 collective-permute-start.1
  5.9 0.7 compare_convert_fusion.weight_ref
  6.5 0.8 subtract_add_fusion
  7.3 0.1 pad_add_fusion.start_ref
  7.4 0.0 collective-permute-done
  7.4 0.3 collective-permute-done.1
  7.8 1.3 pad_add_fusion.1.near_ref
  9.1 0.0 copy-start
  9.1 1.6 copy-done
  10.7 0.0 copy-start.1
  10.7 1.0 copy-done.1
  11.7 0.0 copy-start.2
  11.7 1.0 copy-done.2
  12.8 219.9 %two_minibatches.1 = f32[2,2,256,512]{3,2,1,0:T(8,128)S(1)} custom-call(s32[2,2]{1,0:T(2,128)S(1)} %pad_add_fusion.start_ref, s32[2]{0:T(128)S(1)} %pad_add_fusion.1.near_ref, f32[2,2]{1,0:T(2,128)S(1)} %compare_convert_fusion.weight_ref, f32[2,2,256,512]{3,2,1,0:T(8,128)S(1)} %copy-done, f32[2,256,256]{2,1,0:T(8,128)S(1)} %copy-done.1, ...), custom_call_target="tpu_custom_call" | custom-call | tf_op jit(solution)/shard_map/two_minibatches/pallas_call | solution.py:362
  232.7 1.3 copy.8
Async XLA Ops:
  1.4 6.0 %collective-permute-start = (s32[1]{0:T(128)}, s32[1]{0:T(128)}, u32[]{:S(2)}, u32[]{:S(2)}) collective-permute-start(s32[1]{0:T(128)} %bitcast), channel_id=1, source_target_pairs={{1,0},{2,1},{3,2},{4,3},{5,4},{6,5},{7,6},{9,8},{10,9},{11,10},{12... | collective-permute-start | bytes 20 | tf_op jit(solution)/shard_map/ppermute | solution.py:353
  4.6 3.2 %collective-permute-start.1 = (s32[1]{0:T(128)}, s32[1]{0:T(128)}, u32[]{:S(2)}, u32[]{:S(2)}) collective-permute-start(s32[1]{0:T(128)} %bitcast.1), channel_id=1, source_target_pairs={{0,1},{1,2},{2,3},{3,4},{4,5},{5,6},{6,7},{8,9},{9,10},{10,11},{11... | collective-permute-start | bytes 20 | tf_op jit(solution)/shard_map/ppermute | solution.py:354
  9.1 1.6 copy-start
  10.7 1.0 copy-start.1
  11.7 1.0 copy-start.2

commit v4 on v3

--- a/solution.py
+++ b/solution.py
@@ -13,10 +13,12 @@
 prop_strength = 24.0
 step_rate = 0.08
 MESH = pl.DeviceIdType.MESH
+CHUNK = 128
 VMEM_LIMIT = 48 * 1024 * 1024
 
 
 def operators(extent):
+    order = np.arange(2 * extent).reshape(2, extent // CHUNK, CHUNK).swapaxes(0, 1).reshape(-1)
     counter = np.arange(extent)
     phase = (counter[:, None] * counter[None, :]) % extent
     angles = phase * (2.0 * math.pi / extent)
@@ -28,6 +30,7 @@
     packed = []
     for matrix in (forward, np.conj(forward), fourier, np.conj(fourier)):
         whole = np.block([[matrix.real, matrix.imag], [-matrix.imag, matrix.real]]).astype(np.float32)
+        whole = whole[order][:, order]
         high = whole.astype(ml_dtypes.bfloat16)
         low = (whole - high.astype(np.float32)).astype(ml_dtypes.bfloat16)
         packed.append(np.stack([high, low]))
@@ -43,29 +46,45 @@
     return jnp.dot(first, second, preferred_element_type=jnp.float32)
 
 
-def transform(real, imag, op_ref, which):
+def left_product(real, imag, op_ref, which):
     extent = real.shape[0]
-    real_parts, imag_parts = split(real), split(imag)
+    pieces = range(0, extent, CHUNK)
+    parts = []
+    for r, i in zip(split(real), split(imag)):
+        upper, lower = jnp.concatenate([r, i], 1), jnp.concatenate([-i, r], 1)
+        parts.append(jnp.concatenate([x[at : at + CHUNK] for at in pieces for x in (upper, lower)], 0))
     high, low = [
-        jnp.concatenate([jnp.concatenate([r, i], 1), jnp.concatenate([-i, r], 1)], 0)
-        for r, i in zip(real_parts, imag_parts)
+        jnp.concatenate([op_ref[which, k, 2 * at : 2 * at + CHUNK] for at in pieces], 0) for k in range(2)
     ]
-    left_high, left_low = op_ref[which, 0, :extent], op_ref[which, 1, :extent]
-    turned = dot(left_high, high) + (dot(left_high, low) + dot(left_low, high))
+    return dot(jnp.concatenate([high, high, low], 1), jnp.concatenate([parts[0], parts[1], parts[0]], 0))
+
+
+def transform(get, put, op_ref, which):
+    extent = op_ref.shape[-1] // 2
+    chunks = range(extent // CHUNK)
+    turned = jnp.concatenate([left_product(*get(c), op_ref, which) for c in chunks], 1)
     high, low = split(turned)
-    right_high, right_low = op_ref[which, 0], op_ref[which, 1]
-    out = dot(high, right_high) + (dot(high, right_low) + dot(low, right_high))
-    return out[:, :extent], out[:, extent:]
+    wide = jnp.concatenate([high, high, low], 1)
+    for c in chunks:
+        columns = slice(2 * c * CHUNK, 2 * (c + 1) * CHUNK)
+        right_high, right_low = op_ref[which, 0, :, columns], op_ref[which, 1, :, columns]
+        out = dot(wide, jnp.concatenate([right_high, right_low, right_high], 0))
+        put(c, out[:, :CHUNK], out[:, CHUNK:])
+
+
+def strip_of(c):
+    return slice(c * CHUNK, (c + 1) * CHUNK)
 
 
 def whole_kernel(
     depth_count, tiles, start_ref, near_ref, weight_ref, object_ref, probe_ref, measured_ref, op_ref, strip_ref,
     window, patch_grad, seen, wave_grad, halo_out, halo_in, rim_out, rim_in,
-    wave_send, wave_recv, back_send, back_recv, halo_send, halo_recv, rim_send, rim_recv, turn,
+    wave_send, wave_recv, back_send, back_recv, halo_send, halo_recv, rim_send, rim_recv,
 ):
     phases, slots, _, _, extent, _ = seen.shape
     layers, rows, cols = object_ref.shape[1:]
     half = extent // 2
+    chunks = extent // CHUNK
     area_rows = half + rows
     depth_at = lax.axis_index("depth")
     tile_at = lax.axis_index("tile")
@@ -74,8 +93,6 @@
     has_above = tile_at > 0
     has_below = tile_at < tiles - 1
     own_layers = layers - last
-    parity = tile_at % 2
-    partner = tile_at + 1 - 2 * parity
     links = (
         (not_last, {"depth": depth_at + 1}),
         (depth_at > 0, {"depth": depth_at - 1}),
@@ -110,17 +127,20 @@
 
     pl.semaphore_wait(barrier, 4 - ends)
 
-    def wave_copy(phase, slot):
+    def wave_copy(phase, slot, c):
+        columns = pl.ds(c * CHUNK, CHUNK)
         return pltpu.make_async_remote_copy(
-            src_ref=seen.at[phase, slot, layers], dst_ref=seen.at[phase, slot, 0],
-            send_sem=wave_send.at[phase, slot], recv_sem=wave_recv.at[phase, slot],
+            src_ref=seen.at[phase, slot, layers, :, :, columns], dst_ref=seen.at[phase, slot, 0, :, :, columns],
+            send_sem=wave_send.at[phase, slot, c], recv_sem=wave_recv.at[phase, slot, c],
             device_id=links[0][1], device_id_type=MESH,
         )
 
-    def back_copy(phase, slot):
+    def back_copy(phase, slot, c):
+        columns = pl.ds(c * CHUNK, CHUNK)
         return pltpu.make_async_remote_copy(
-            src_ref=wave_grad.at[phase, slot, 0], dst_ref=wave_grad.at[phase, slot, layers],
-            send_sem=back_send.at[phase, slot], recv_sem=back_recv.at[phase, slot],
+            src_ref=wave_grad.at[phase, slot, 0, :, :, columns],
+            dst_ref=wave_grad.at[phase, slot, layers, :, :, columns],
+            send_sem=back_send.at[phase, slot, c], recv_sem=back_recv.at[phase, slot, c],
             device_id=links[1][1], device_id_type=MESH,
         )
 
@@ -182,88 +202,81 @@
             piece = jnp.concatenate([piece, jnp.zeros((half, cols - extent), jnp.float32)], 1)
             strip_ref[part, layer, base : base + half] -= pltpu.roll(piece, near_ref[side], 1)
 
-    def illuminated(phase, slot, layer):
-        o_real, o_imag = window[slot, 0, layer], window[slot, 1, layer]
-        w_real, w_imag = seen[phase, slot, layer, 0], seen[phase, slot, layer, 1]
+    def illuminated(phase, slot, layer, c):
+        at = strip_of(c)
+        o_real, o_imag = window[slot, 0, layer, :, at], window[slot, 1, layer, :, at]
+        w_real, w_imag = seen[phase, slot, layer, 0, :, at], seen[phase, slot, layer, 1, :, at]
         return o_real * w_real - o_imag * w_imag, o_real * w_imag + o_imag * w_real
 
-    def keep_gradients(phase, slot, layer, g_real, g_imag):
-        o_real, o_imag = window[slot, 0, layer], window[slot, 1, layer]
-        w_real, w_imag = seen[phase, slot, layer, 0], seen[phase, slot, layer, 1]
-        wave_grad[phase, slot, layer, 0] = g_real * o_real + g_imag * o_imag
-        wave_grad[phase, slot, layer, 1] = g_imag * o_real - g_real * o_imag
-        patch_grad[slot, 0, layer] = g_real * w_real + g_imag * w_imag
-        patch_grad[slot, 1, layer] = g_imag * w_real - g_real * w_imag
-
-    def pass_turn(phase, slot):
-        wave_copy(phase, slot).wait_send()
-
-        @pl.when((parity == 0) | (slot < slots - 1))
-        def _():
-            pl.semaphore_signal(turn, inc=1, device_id={"tile": partner}, device_id_type=MESH)
-
-    def send_in_turn(phase, slot):
-        @pl.when(slot > 0)
-        def _():
-            pass_turn(phase, slot - 1)
-
-        @pl.when((parity == 1) | (slot > 0))
-        def _():
-            pl.semaphore_wait(turn, 1)
-
-        wave_copy(phase, slot).start()
-
-        @pl.when(slot == slots - 1)
-        def _():
-            pass_turn(phase, slot)
+    def keep_gradients(phase, slot, layer, c, g_real, g_imag):
+        at = strip_of(c)
+        o_real, o_imag = window[slot, 0, layer, :, at], window[slot, 1, layer, :, at]
+        w_real, w_imag = seen[phase, slot, layer, 0, :, at], seen[phase, slot, layer, 1, :, at]
+        wave_grad[phase, slot, layer, 0, :, at] = g_real * o_real + g_imag * o_imag
+        wave_grad[phase, slot, layer, 1, :, at] = g_imag * o_real - g_real * o_imag
+        patch_grad[slot, 0, layer, :, at] = g_real * w_real + g_imag * w_imag
+        patch_grad[slot, 1, layer, :, at] = g_imag * w_real - g_real * w_imag
 
     def go_out(phase, slot):
         @pl.when(depth_at == 0)
         def _():
             seen[phase, slot, 0] = probe_ref[...]
 
-        @pl.when(depth_at > 0)
-        def _():
-            wave_copy(phase, slot).wait_recv()
-
         @pl.loop(0, own_layers)
         def _(layer):
-            real, imag = transform(*illuminated(phase, slot, layer), op_ref, 0)
-            seen[phase, slot, layer + 1, 0] = real
-            seen[phase, slot, layer + 1, 1] = imag
-
-        @pl.when(depth_at == 0)
-        def _():
-            send_in_turn(phase, slot)
-
-        @pl.when(not_last & (depth_at > 0))
-        def _():
-            wave_copy(phase, slot).start()
+            def get(c):
+                @pl.when((layer == 0) & (depth_at > 0))
+                def _():
+                    wave_copy(phase, slot, c).wait_recv()
+
+                return illuminated(phase, slot, layer, c)
+
+            def put(c, real, imag):
+                seen[phase, slot, layer + 1, 0, :, strip_of(c)] = real
+                seen[phase, slot, layer + 1, 1, :, strip_of(c)] = imag
+
+                @pl.when((layer == layers - 1) & not_last)
+                def _():
+                    wave_copy(phase, slot, c).start()
+
+            transform(get, put, op_ref, 0)
 
         @pl.when(last == 1)
         def _():
-            real, imag = transform(*illuminated(phase, slot, layers - 1), op_ref, 2)
-            resid = real * real + imag * imag - measured_ref[slot]
-            factor = (4.0 * weight_ref[phase, slot]) * resid
-            g_real, g_imag = transform(factor * real, factor * imag, op_ref, 3)
-            keep_gradients(phase, slot, layers - 1, g_real, g_imag)
+            if layers == 1:
+                for c in range(chunks):
+                    wave_copy(phase, slot, c).wait_recv()
+            far = {}
+
+            def keep(c, real, imag):
+                resid = real * real + imag * imag - measured_ref[slot, :, strip_of(c)]
+                factor = (4.0 * weight_ref[phase, slot]) * resid
+                far[c] = (factor * real, factor * imag)
+
+            transform(functools.partial(illuminated, phase, slot, layers - 1), keep, op_ref, 2)
+            transform(far.get, functools.partial(keep_gradients, phase, slot, layers - 1), op_ref, 3)
 
     def go_back(phase, slot):
-        @pl.when(not_last)
-        def _():
-            back_copy(phase, slot).wait_recv()
-
         @pl.loop(0, own_layers)
         def _(step):
             layer = own_layers - 1 - step
-            g_real, g_imag = transform(
-                wave_grad[phase, slot, layer + 1, 0], wave_grad[phase, slot, layer + 1, 1], op_ref, 1
-            )
-            keep_gradients(phase, slot, layer, g_real, g_imag)
-
-        @pl.when(depth_at > 0)
-        def _():
-            back_copy(phase, slot).start()
+
+            def get(c):
+                @pl.when((layer == layers - 1) & not_last)
+                def _():
+                    back_copy(phase, slot, c).wait_recv()
+
+                at = strip_of(c)
+                return wave_grad[phase, slot, layer + 1, 0, :, at], wave_grad[phase, slot, layer + 1, 1, :, at]
+
+            def put(c, g_real, g_imag):
+                keep_gradients(phase, slot, layer, c, g_real, g_imag)
+
+                @pl.when((layer == 0) & (depth_at > 0))
+                def _():
+                    back_copy(phase, slot, c).start()
+
+            transform(get, put, op_ref, 1)
 
     @pl.loop(0, layers)
     def _(layer):
@@ -318,13 +331,15 @@
     def _(phase):
         for slot in range(2):
 
-            @pl.when(not_last & (depth_at > 0))
-            def _():
-                wave_copy(phase, slot).wait_send()
-
-            @pl.when(depth_at > 0)
-            def _():
-                back_copy(phase, slot).wait_send()
+            for c in range(chunks):
+
+                @pl.when(not_last)
+                def _():
+                    wave_copy(phase, slot, c).wait_send()
+
+                @pl.when(depth_at > 0)
+                def _():
+                    back_copy(phase, slot, c).wait_send()
 
             @pl.loop(0, layers)
             def _(layer):
@@ -365,9 +380,8 @@
         in_specs=[scalars, scalars, scalars, whole, whole, whole, whole],
         out_specs=whole,
         scratch_shapes=[patches, patches, waves, waves, edge, edge, edge, edge]
-        + [pltpu.SemaphoreType.DMA((phases, slots))] * 4
-        + [pltpu.SemaphoreType.DMA((phases, slots, layers))] * 4
-        + [pltpu.SemaphoreType.REGULAR],
+        + [pltpu.SemaphoreType.DMA((phases, slots, extent // CHUNK))] * 4
+        + [pltpu.SemaphoreType.DMA((phases, slots, layers))] * 4,
         compiler_params=pltpu.CompilerParams(
             collective_id=0, has_side_effects=True, vmem_limit_bytes=VMEM_LIMIT
         ),

time: 234 us -> 254 us (1.085)
  the two profiles are of different devices: /device:TPU:7 before, /device:TPU:3 now
where the time goes in v4:
time: 254 us; the launch traced here: 250 us
  Pallas kernels  234 us (92%)
  starting transfers between devices  6.45 us (3%)
  local copies, waits for them, and re-layouts  6.41 us (3%)
  other arithmetic  2.88 us (1%)
    pallas_call x1, Pallas kernels, shards(): pl.pallas_call(functools.partial(whole_kernel, depth_count, tiles), out_s...  234 us
  transfers between devices with their start and end apart: 2, of which 0 were waited for; matrix products, arithmetic and copies ran while one was open for 1% of the time, Pallas kernels for 0%

profile of v4, /device:TPU:3, one launch (start us, length us, event | category | flops | bytes accessed | tf_op | source)
XLA Modules:
  0.0 249.9 jit_solution(11620147167130339453)
XLA Ops:
  0.0 1.4 fusion
  1.4 2.6 %collective-permute-start = (s32[1]{0:T(128)}, s32[1]{0:T(128)}, u32[]{:S(2)}, u32[]{:S(2)}) collective-permute-start(s32[1]{0:T(128)} %bitcast), channel_id=1, source_target_pairs={{1,0},{2,1},{3,2},{4,3},{5,4},{6,5},{7,6},{9,8},{10,9},{11,10},{12... | collective-permute-start | bytes 20 | tf_op jit(solution)/shard_map/ppermute | solution.py:368
  4.0 3.9 %collective-permute-start.1 = (s32[1]{0:T(128)}, s32[1]{0:T(128)}, u32[]{:S(2)}, u32[]{:S(2)}) collective-permute-start(s32[1]{0:T(128)} %bitcast.1), channel_id=1, source_target_pairs={{0,1},{1,2},{2,3},{3,4},{4,5},{5,6},{6,7},{8,9},{9,10},{10,11},{11... | collective-permute-start | bytes 20 | tf_op jit(solution)/shard_map/ppermute | solution.py:369
  7.9 0.7 compare_convert_fusion.weight_ref
  8.6 0.8 subtract_add_fusion
  9.4 0.1 pad_add_fusion.start_ref
  9.5 0.0 collective-permute-done
  9.5 0.0 collective-permute-done.1
  9.5 1.3 pad_add_fusion.1.near_ref
  10.8 0.0 copy-start
  10.8 1.6 copy-done
  12.4 0.0 copy-start.1
  12.4 1.0 copy-done.1
  13.4 0.0 copy-start.2
  13.4 1.0 copy-done.2
  14.5 234.1 %two_minibatches.1 = f32[2,2,256,512]{3,2,1,0:T(8,128)S(1)} custom-call(s32[2,2]{1,0:T(2,128)S(1)} %pad_add_fusion.start_ref, s32[2]{0:T(128)S(1)} %pad_add_fusion.1.near_ref, f32[2,2]{1,0:T(2,128)S(1)} %compare_convert_fusion.weight_ref, f32[2,2,256,512]{3,2,1,0:T(8,128)S(1)} %copy-done, f32[2,256,256]{2,1,0:T(8,128)S(1)} %copy-done.1, ...), custom_call_target="tpu_custom_call" | custom-call | tf_op jit(solution)/shard_map/two_minibatches/pallas_call | solution.py:377
  248.6 1.3 copy.8
Async XLA Ops:
  1.4 8.0 %collective-permute-start = (s32[1]{0:T(128)}, s32[1]{0:T(128)}, u32[]{:S(2)}, u32[]{:S(2)}) collective-permute-start(s32[1]{0:T(128)} %bitcast), channel_id=1, source_target_pairs={{1,0},{2,1},{3,2},{4,3},{5,4},{6,5},{7,6},{9,8},{10,9},{11,10},{12... | collective-permute-start | bytes 20 | tf_op jit(solution)/shard_map/ppermute | solution.py:368
  4.0 5.5 %collective-permute-start.1 = (s32[1]{0:T(128)}, s32[1]{0:T(128)}, u32[]{:S(2)}, u32[]{:S(2)}) collective-permute-start(s32[1]{0:T(128)} %bitcast.1), channel_id=1, source_target_pairs={{0,1},{1,2},{2,3},{3,4},{4,5},{5,6},{6,7},{8,9},{9,10},{10,11},{11... | collective-permute-start | bytes 20 | tf_op jit(solution)/shard_map/ppermute | solution.py:369
  10.8 1.6 copy-start
  12.4 1.0 copy-start.1
  13.4 1.0 copy-start.2
